TPU v7x, 32 devices: a whole 2x2x4 slice. The times are simulated.
32 devices in a mesh: row: 4 (over y, x), col: 8 (over z, core).
Axes of the slice: x: 2, y: 2, z: 4, core: 2. Of those that a mesh axis runs over, the one named last changes fastest.
Arguments:
- a_blocks: bfloat16 [8, 128, 128, 128], P('col', 'row'), may hold values from -0.5 to 0.5
- a_rows: int32 [8, 128], P('col', 'row'), may hold values from 0 to 7, as said below
- b_blocks: bfloat16 [4, 128, 128, 128], P('row', 'col'), may hold values from -6 to 6
- b_cols: int32 [4, 128], P('row', 'col'), may hold values from 0 to 15, as said below
- c_keep: int32 [4, 8, 24], P('row', 'col'), may hold values from 0 to 127, as said below
- c_owner: int32 [4, 8, 24], P('row', 'col'), may hold values from 0 to 31, as said below
- c_slot: int32 [4, 8, 24], P('row', 'col'), may hold values from 0 to 63, as said below
Outputs:
- owned_blocks: bfloat16 [4, 512, 128, 128], P('row', 'col')
Inputs may be any that keep to these rules, and one draw needn't show every extreme that they name: `a_rows`: for each j, i and block column c of the panel, the slots c * (2) to (c + 1) * 2 - 1 name 2 distinct rows. `b_cols`: for each i, j and block row of the half panel, its 2 consecutive slots name distinct columns. `c_keep`: the 24 positions of one device are distinct. `c_owner`: each device sends to exactly 12 distinct owners, exactly 2 blocks to each; some owner receives 64 blocks in all, none more. `c_slot`: the pairs (owner, slot) are distinct over all kept blocks of all devices.
All inputs are finite; a program needn't handle non-finite values.
Results may differ from a plain program's by a relative error of at most 0.001.
Values may be sent and summed in bfloat16 or wider, within the bound.
No kernel may reach another device: no remote copies, remote signals or barrier semaphores. Data moves between devices by JAX's collectives and lax.ppermute only.
A program may use at most 128 MiB of HBM per device.

v0:
```python
import jax
import jax.numpy as jnp
from jax import lax
from jax.sharding import PartitionSpec as P

RB = 8
SCAP = 2


def passed_along(shard, axis, by):
    devices = lax.axis_size(axis)
    return lax.ppermute(shard, axis, [(i, (i + by) % devices) for i in range(devices)])


def add_products(accumulated, a_panel, row_ids, b_panel, col_ids, panel_width):
    block_size = a_panel.shape[-1]
    left_blocks = a_panel.reshape(panel_width, -1, block_size, block_size)
    right_blocks = b_panel.reshape(panel_width, -1, block_size, block_size)
    products = jnp.einsum(
        "kaxy,kbyz->kabxz", left_blocks, right_blocks, preferred_element_type=jnp.float32
    )
    targets = (
        row_ids.reshape(panel_width, -1)[:, :, None] * panel_width
        + col_ids.reshape(panel_width, -1)[:, None, :]
    )
    return accumulated.at[targets.reshape(-1)].add(products.reshape(-1, block_size, block_size))


def join_halves(b_half, b_half_index, other_half, other_index, row_count):
    upper_half = lax.axis_index("col") >= row_count
    b_panel = jnp.where(
        upper_half,
        jnp.concatenate([other_half, b_half], axis=0),
        jnp.concatenate([b_half, other_half], axis=0),
    )
    b_index = jnp.where(
        upper_half,
        jnp.concatenate([other_index, b_half_index], axis=0),
        jnp.concatenate([b_half_index, other_index], axis=0),
    )
    return (b_panel, b_index)


def body(a_blocks, a_rows, b_blocks, b_cols, c_keep, c_owner, c_slot):
    row_count = lax.axis_size("row")
    col_count = lax.axis_size("col")
    panel_width = RB * col_count // row_count
    region_size = RB * panel_width
    block_size = a_blocks.shape[-1]
    a_panel = a_blocks[0]
    a_index = a_rows[0]
    b_half = b_blocks[0]
    b_half_index = b_cols[0]
    accumulated = jnp.zeros((region_size, block_size, block_size), jnp.float32)
    other_half, other_index = passed_along((b_half, b_half_index), "col", row_count)
    b_panel, b_index = join_halves(b_half, b_half_index, other_half, other_index, row_count)
    accumulated = add_products(accumulated, a_panel, a_index, b_panel, b_index, panel_width)
    moving_a, moving_rows = (a_panel, a_index)
    moving_b, moving_cols = (b_panel, b_index)
    for offset in range(1, row_count):
        moving_a, moving_rows = passed_along((moving_a, moving_rows), "row", -1)
        moving_b, moving_cols = passed_along((moving_b, moving_cols), "col", -1)
        accumulated = add_products(
            accumulated, moving_a, moving_rows, moving_b, moving_cols, panel_width
        )
    keep_list = c_keep[0, 0]
    owner_ids = c_owner[0, 0]
    slot_ids = c_slot[0, 0]
    kept_blocks = accumulated[keep_list].astype(jnp.bfloat16)
    counter = jnp.arange(keep_list.shape[0], dtype=jnp.int32)
    earlier = (owner_ids[:, None] == owner_ids[None, :]) & (counter[None, :] < counter[:, None])
    bucket_pos = owner_ids * SCAP + jnp.sum(earlier.astype(jnp.int32), axis=1)
    device_count = row_count * col_count
    capacity = 2 * device_count
    send_blocks = (
        jnp.zeros((device_count * SCAP, block_size, block_size), jnp.bfloat16)
        .at[bucket_pos]
        .set(kept_blocks)
    )
    send_slots = jnp.full((device_count * SCAP,), capacity, jnp.int32).at[bucket_pos].set(slot_ids)
    recv_blocks, recv_slots = (
        lax.all_to_all(send_blocks, ("row", "col"), split_axis=0, concat_axis=0, tiled=True),
        lax.all_to_all(send_slots, ("row", "col"), split_axis=0, concat_axis=0, tiled=True),
    )
    owned_blocks = jnp.zeros((capacity, block_size, block_size), jnp.bfloat16)
    owned_blocks = owned_blocks.at[recv_slots].set(recv_blocks, mode="drop")
    return owned_blocks[None]


def solution(mesh):
    return jax.shard_map(
        body,
        mesh=mesh,
        in_specs=(
            P("col", "row", None, None),
            P("col", "row"),
            P("row", "col", None, None),
            P("row", "col"),
            P("row", "col", None),
            P("row", "col", None),
            P("row", "col", None),
        ),
        out_specs=P("row", "col", None, None),
        check_vma=False,
    )
```

profile of v0, /device:TPU:0, one launch (start us, length us, event | category | flops | bytes accessed | tf_op | source)
XLA Modules:
  0.0 247.6 jit_solution(5785818849860998843)
XLA Ops:
  0.0 4.0 %collective-permute-start.1 = (bf16[16,128,128]{2,1,0:T(8,128)(2,1)}, bf16[16,128,128]{2,1,0:T(8,128)(2,1)S(1)}, u32[]{:S(2)}, u32[]{:S(2)}) collective-permute-start(bf16[16,128,128]{2,1,0:T(8,128)(2,1)} %bitcast.103), channel_id=1, source_target_pairs={{0,4},{1,5},{2,6},{3,7},{4,0},{5,1},{6,2},{7,3},{8,12},{9,13},{10,... | collective-permute-start | bytes 1572872 | tf_op jit(solution)/shard_map/ppermute | solution.py:12
  10.4 4.9 %all-to-all-start = ((s32[32,2,1]{1,2,0:T(1,128)}), s32[32,2,1]{1,2,0:T(1,128)S(1)}, u32[]{:S(2)}, u32[]{:S(2)}) async-start(s32[32,2,1]{1,2,0:T(1,128)} %bitcast.5), calls=%async_computation | async-start | bytes 32768 | tf_op jit(solution)/shard_map/all_to_all | solution.py:83
  18.7 9.0 %collective-permute-done = s32[16]{0:T(128)S(1)} collective-permute-done((s32[16]{0:T(128)}, s32[16]{0:T(128)S(1)}, u32[]{:S(2)}, u32[]{:S(2)}) %collective-permute-start) | collective-permute-done | bytes 96 | tf_op jit(solution)/shard_map/ppermute | solution.py:12
  36.8 8.3 %collective-permute-done.3 = s32[32]{0:T(128)S(1)} collective-permute-done((s32[32]{0:T(128)S(1)}, s32[32]{0:T(128)S(1)}, u32[]{:S(2)}, u32[]{:S(2)}) %collective-permute-start.3) | collective-permute-done | bytes 160 | tf_op jit(solution)/shard_map/ppermute | solution.py:12
  45.4 3.8 %collective-permute-start.7 = (s32[32]{0:T(128)S(1)}, s32[32]{0:T(128)S(1)}, u32[]{:S(2)}, u32[]{:S(2)}) collective-permute-start(s32[32]{0:T(128)S(1)} %collective-permute-done.3), channel_id=1, source_target_pairs={{0,7},{1,0},{2,1},{3,2},{4,3},{5,4},{6,5},{7,6},{8,15},{9,8},{10,9... | collective-permute-start | bytes 392 | tf_op jit(solution)/shard_map/ppermute | solution.py:12
  53.1 3.2 %collective-permute-start.8 = (bf16[32,128,128]{2,1,0:T(8,128)(2,1)S(1)}, bf16[32,128,128]{2,1,0:T(8,128)(2,1)}, u32[]{:S(2)}, u32[]{:S(2)}) collective-permute-start(bf16[32,128,128]{2,1,0:T(8,128)(2,1)S(1)} %collective-permute-done.4), channel_id=1, source_target_pairs={{0,7},{1,0},{2,1},{3,2},{4,3},{5,4},{6,5},{7,6},{8,15},{9,8},{10,9... | collective-permute-start | bytes 3145736 | tf_op jit(solution)/shard_map/ppermute | solution.py:12
  56.6 12.0 %collective-permute-done.11 = s32[32]{0:T(128)S(1)} collective-permute-done((s32[32]{0:T(128)S(1)}, s32[32]{0:T(128)S(1)}, u32[]{:S(2)}, u32[]{:S(2)}) %collective-permute-start.11) | collective-permute-done | bytes 160 | tf_op jit(solution)/shard_map/ppermute | solution.py:12
  68.9 6.1 %collective-permute-done.9 = bf16[32,128,128]{2,1,0:T(8,128)(2,1)} collective-permute-done((bf16[32,128,128]{2,1,0:T(8,128)(2,1)S(1)}, bf16[32,128,128]{2,1,0:T(8,128)(2,1)}, u32[]{:S(2)}, u32[]{:S(2)}) %collective-permute-start.9) | collective-permute-done | bytes 1048608 | tf_op jit(solution)/shard_map/ppermute | solution.py:12
  79.0 3.9 %convolution_bitcast_fusion.3 = f32[16,2,2,128,128]{3,4,1,2,0:T(8,128)} fusion(bf16[16,2,128,128,1]{3,2,4,1,0:T(8,128)(2,1)S(1)} %bitcast.98, bf16[16,2,128,128,1]{3,2,1,4,0:T(8,128)(2,1)} %bitcast.100), kind=kOutput, calls=%fused_computation.11 | convolution fusion | flops 268435456 | bytes 6291456 | tf_op jit(solution)/shard_map/kaxy,kbyz->kabxz/dot_general | solution.py:19
  82.9 5.3 %copy.41 = f32[16,2,2,128,128]{4,3,2,1,0:T(8,128)} copy(f32[16,2,2,128,128]{3,4,1,2,0:T(8,128)} %convolution_bitcast_fusion.3) | data formatting | bytes 8388608 | tf_op jit(solution)/shard_map/kaxy,kbyz->kabxz/transpose | solution.py:19
  88.2 4.3 %broadcast_in_dim.4 = f32[128,128,128]{2,1,0:T(8,128)} broadcast(f32[]{:T(128)} %constant.13.clone.1), dimensions={} | broadcast | bytes 8388612 | tf_op jit(solution)/shard_map/broadcast_in_dim | solution.py:54
  92.5 13.5 %scatter_fusion = f32[128,128,128]{2,1,0:T(8,128)} fusion(f32[128,128,128]{2,1,0:T(8,128)} %broadcast_in_dim.4, s32[64]{0:T(128)S(1)} %fusion.3, f32[64,128,128]{2,1,0:T(8,128)} %bitcast.94), kind=kCustom, calls=%fused_computation.2 | custom fusion | flops 1048576 | bytes 12583168 | tf_op jit(solution)/shard_map/scatter-add | solution.py:26
  108.7 5.3 %copy.43 = f32[16,2,2,128,128]{4,3,2,1,0:T(8,128)} copy(f32[16,2,2,128,128]{3,4,1,2,0:T(8,128)} %convolution_bitcast_fusion.2) | data formatting | bytes 8388608 | tf_op jit(solution)/shard_map/kaxy,kbyz->kabxz/transpose | solution.py:19
  114.0 13.5 %scatter_fusion.1 = f32[128,128,128]{2,1,0:T(8,128)} fusion(f32[128,128,128]{2,1,0:T(8,128)} %scatter_fusion, s32[64]{0:T(128)S(1)} %fusion.4, f32[64,128,128]{2,1,0:T(8,128)} %bitcast.95), kind=kCustom, calls=%fused_computation.3 | custom fusion | flops 1048576 | bytes 12583168 | tf_op jit(solution)/shard_map/scatter-add | solution.py:26
  127.6 4.3 %convolution_bitcast_fusion.1 = f32[16,2,2,128,128]{3,4,1,2,0:T(8,128)} fusion(bf16[16,2,128,128,1]{3,2,4,1,0:T(8,128)(2,1)} %bitcast.67, bf16[16,2,128,128,1]{3,2,1,4,0:T(8,128)(2,1)} %bitcast.34), kind=kOutput, calls=%fused_computation.9 | convolution fusion | flops 268435456 | bytes 6291456 | tf_op jit(solution)/shard_map/kaxy,kbyz->kabxz/dot_general | solution.py:19
  131.8 5.3 %copy.45 = f32[16,2,2,128,128]{4,3,2,1,0:T(8,128)} copy(f32[16,2,2,128,128]{3,4,1,2,0:T(8,128)} %convolution_bitcast_fusion.1) | data formatting | bytes 8388608 | tf_op jit(solution)/shard_map/kaxy,kbyz->kabxz/transpose | solution.py:19
  137.2 13.5 %scatter_fusion.2 = f32[128,128,128]{2,1,0:T(8,128)} fusion(f32[128,128,128]{2,1,0:T(8,128)} %scatter_fusion.1, s32[64]{0:T(128)S(1)} %fusion.5, f32[64,128,128]{2,1,0:T(8,128)} %bitcast.96), kind=kCustom, calls=%fused_computation.4 | custom fusion | flops 1048576 | bytes 12583168 | tf_op jit(solution)/shard_map/scatter-add | solution.py:26
  150.7 4.3 %convolution_bitcast_fusion = f32[16,2,2,128,128]{3,4,1,2,0:T(8,128)} fusion(bf16[16,2,128,128,1]{3,2,4,1,0:T(8,128)(2,1)} %bitcast.68, bf16[16,2,128,128,1]{3,2,1,4,0:T(8,128)(2,1)} %bitcast.43), kind=kOutput, calls=%fused_computation.8 | convolution fusion | flops 268435456 | bytes 6291456 | tf_op jit(solution)/shard_map/kaxy,kbyz->kabxz/dot_general | solution.py:19
  155.0 5.4 %copy.47 = f32[16,2,2,128,128]{4,3,2,1,0:T(8,128)} copy(f32[16,2,2,128,128]{3,4,1,2,0:T(8,128)} %convolution_bitcast_fusion) | data formatting | bytes 8388608 | tf_op jit(solution)/shard_map/kaxy,kbyz->kabxz/transpose | solution.py:19
  160.3 13.6 %scatter_fusion.3 = f32[128,128,128]{2,1,0:T(8,128)} fusion(f32[128,128,128]{2,1,0:T(8,128)} %scatter_fusion.2, s32[64]{0:T(128)S(1)} %fusion.6, f32[64,128,128]{2,1,0:T(8,128)} %bitcast.97), kind=kCustom, calls=%fused_computation.5 | custom fusion | flops 1048576 | bytes 12583168 | tf_op jit(solution)/shard_map/scatter-add | solution.py:26
  174.0 4.1 %gather_fusion = bf16[24,128,128]{2,1,0:T(8,128)(2,1)S(1)} fusion(f32[128,128,128]{2,1,0:T(8,128)} %scatter_fusion.3, s32[1024]{0:T(1024)S(1)} %pad_clamp_fusion), kind=kCustom, calls=%fused_computation | custom fusion | bytes 1572960 | tf_op jit(solution)/shard_map/gather | solution.py:69
  179.8 4.5 %scatter_fusion.4 = bf16[64,128,128]{2,1,0:T(8,128)(2,1)} fusion(bf16[64,128,128]{2,1,0:T(8,128)(2,1)} %broadcast.178.clone, s32[24]{0:T(128)S(1)} %fusion.1, bf16[24,128,128]{2,1,0:T(8,128)(2,1)S(1)} %gather_fusion), kind=kCustom, calls=%fused_computation.6 | custom fusion | bytes 2359392 | tf_op jit(solution)/shard_map/scatter | solution.py:78
  187.9 49.3 %all-to-all-done.1 = bf16[64,128,128]{2,1,0:T(8,128)(2,1)S(1)} async-done(((bf16[64,128,128]{2,1,0:T(8,128)(2,1)}), bf16[64,128,128]{2,1,0:T(8,128)(2,1)S(1)}, u32[]{:S(2)}, u32[]{:S(2)}) %all-to-all-start.1) | async-done | bytes 2097184 | tf_op jit(solution)/shard_map/all_to_all | solution.py:82
  239.1 8.6 %scatter_fusion.5 = bf16[64,128,128]{2,1,0:T(8,128)(2,1)} fusion(bf16[64,128,128]{2,1,0:T(8,128)(2,1)} %broadcast.178, s32[64]{0:T(128)S(1)} %fusion.2, bf16[64,128,128]{2,1,0:T(8,128)(2,1)S(1)} %all-to-all-done.1), kind=kCustom, calls=%fused_computation.7 | custom fusion | bytes 6291712 | tf_op jit(solution)/shard_map/scatter | solution.py:86
  (68 shorter events, 37.3 us)
Async XLA Ops:
  0.0 28.3 %collective-permute-start.1 = (bf16[16,128,128]{2,1,0:T(8,128)(2,1)}, bf16[16,128,128]{2,1,0:T(8,128)(2,1)S(1)}, u32[]{:S(2)}, u32[]{:S(2)}) collective-permute-start(bf16[16,128,128]{2,1,0:T(8,128)(2,1)} %bitcast.103), channel_id=1, source_target_pairs={{0,4},{1,5},{2,6},{3,7},{4,0},{5,1},{6,2},{7,3},{8,12},{9,13},{10,... | collective-permute-start | bytes 1572872 | tf_op jit(solution)/shard_map/ppermute | solution.py:12
  4.0 23.7 %collective-permute-start = (s32[16]{0:T(128)}, s32[16]{0:T(128)S(1)}, u32[]{:S(2)}, u32[]{:S(2)}) collective-permute-start(s32[16]{0:T(128)} %bitcast.105), channel_id=1, source_target_pairs={{0,4},{1,5},{2,6},{3,7},{4,0},{5,1},{6,2},{7,3},{8,12},{9,13},{10,... | collective-permute-start | bytes 200 | tf_op jit(solution)/shard_map/ppermute | solution.py:12
  4.1 47.8 %collective-permute-start.5 = (bf16[32,128,128]{2,1,0:T(8,128)(2,1)}, bf16[32,128,128]{2,1,0:T(8,128)(2,1)S(1)}, u32[]{:S(2)}, u32[]{:S(2)}) collective-permute-start(bf16[32,128,128]{2,1,0:T(8,128)(2,1)} %bitcast.99), channel_id=1, source_target_pairs={{0,24},{8,0},{16,8},{24,16},{1,25},{9,1},{17,9},{25,17},{2,26},{10... | collective-permute-start | bytes 3145736 | tf_op jit(solution)/shard_map/ppermute | solution.py:12
  6.8 27.4 %collective-permute-start.2 = (s32[32]{0:T(128)}, s32[32]{0:T(128)S(1)}, u32[]{:S(2)}, u32[]{:S(2)}) collective-permute-start(s32[32]{0:T(128)} %bitcast.109), channel_id=1, source_target_pairs={{0,24},{8,0},{16,8},{24,16},{1,25},{9,1},{17,9},{25,17},{2,26},{10... | collective-permute-start | bytes 392 | tf_op jit(solution)/shard_map/ppermute | solution.py:12
  10.4 174.0 %all-to-all-start = ((s32[32,2,1]{1,2,0:T(1,128)}), s32[32,2,1]{1,2,0:T(1,128)S(1)}, u32[]{:S(2)}, u32[]{:S(2)}) async-start(s32[32,2,1]{1,2,0:T(1,128)} %bitcast.5), calls=%async_computation | async-start | bytes 32768 | tf_op jit(solution)/shard_map/all_to_all | solution.py:83
  29.7 23.4 %collective-permute-start.4 = (bf16[32,128,128]{2,1,0:T(8,128)(2,1)S(1)}, bf16[32,128,128]{2,1,0:T(8,128)(2,1)S(1)}, u32[]{:S(2)}, u32[]{:S(2)}) collective-permute-start(bf16[32,128,128]{2,1,0:T(8,128)(2,1)S(1)} %maximum_select_fusion), channel_id=1, source_target_pairs={{0,7},{1,0},{2,1},{3,2},{4,3},{5,4},{6,5},{7,6},{8,15},{9,8},{10,9... | collective-permute-start | bytes 3145736 | tf_op jit(solution)/shard_map/ppermute | solution.py:12
  33.6 11.5 %collective-permute-start.3 = (s32[32]{0:T(128)S(1)}, s32[32]{0:T(128)S(1)}, u32[]{:S(2)}, u32[]{:S(2)}) collective-permute-start(s32[32]{0:T(128)S(1)} %broadcast_select_fusion), channel_id=1, source_target_pairs={{0,7},{1,0},{2,1},{3,2},{4,3},{5,4},{6,5},{7,6},{8,15},{9,8},{10,9... | collective-permute-start | bytes 392 | tf_op jit(solution)/shard_map/ppermute | solution.py:12
  34.3 14.9 %collective-permute-start.6 = (s32[32]{0:T(128)S(1)}, s32[32]{0:T(128)S(1)}, u32[]{:S(2)}, u32[]{:S(2)}) collective-permute-start(s32[32]{0:T(128)S(1)} %collective-permute-done.2), channel_id=1, source_target_pairs={{0,24},{8,0},{16,8},{24,16},{1,25},{9,1},{17,9},{25,17},{2,26},{10... | collective-permute-start | bytes 392 | tf_op jit(solution)/shard_map/ppermute | solution.py:12
  45.4 6.3 %collective-permute-start.7 = (s32[32]{0:T(128)S(1)}, s32[32]{0:T(128)S(1)}, u32[]{:S(2)}, u32[]{:S(2)}) collective-permute-start(s32[32]{0:T(128)S(1)} %collective-permute-done.3), channel_id=1, source_target_pairs={{0,7},{1,0},{2,1},{3,2},{4,3},{5,4},{6,5},{7,6},{8,15},{9,8},{10,9... | collective-permute-start | bytes 392 | tf_op jit(solution)/shard_map/ppermute | solution.py:12
  49.3 7.3 %collective-permute-start.10 = (s32[32]{0:T(128)S(1)}, s32[32]{0:T(128)S(1)}, u32[]{:S(2)}, u32[]{:S(2)}) collective-permute-start(s32[32]{0:T(128)S(1)} %collective-permute-done.6), channel_id=1, source_target_pairs={{0,24},{8,0},{16,8},{24,16},{1,25},{9,1},{17,9},{25,17},{2,26},{10... | collective-permute-start | bytes 392 | tf_op jit(solution)/shard_map/ppermute | solution.py:12
  51.8 23.2 %collective-permute-start.9 = (bf16[32,128,128]{2,1,0:T(8,128)(2,1)S(1)}, bf16[32,128,128]{2,1,0:T(8,128)(2,1)}, u32[]{:S(2)}, u32[]{:S(2)}) collective-permute-start(bf16[32,128,128]{2,1,0:T(8,128)(2,1)S(1)} %collective-permute-done.5), channel_id=1, source_target_pairs={{0,24},{8,0},{16,8},{24,16},{1,25},{9,1},{17,9},{25,17},{2,26},{10... | collective-permute-start | bytes 3145736 | tf_op jit(solution)/shard_map/ppermute | solution.py:12
  53.1 23.1 %collective-permute-start.8 = (bf16[32,128,128]{2,1,0:T(8,128)(2,1)S(1)}, bf16[32,128,128]{2,1,0:T(8,128)(2,1)}, u32[]{:S(2)}, u32[]{:S(2)}) collective-permute-start(bf16[32,128,128]{2,1,0:T(8,128)(2,1)S(1)} %collective-permute-done.4), channel_id=1, source_target_pairs={{0,7},{1,0},{2,1},{3,2},{4,3},{5,4},{6,5},{7,6},{8,15},{9,8},{10,9... | collective-permute-start | bytes 3145736 | tf_op jit(solution)/shard_map/ppermute | solution.py:12
  56.5 12.1 %collective-permute-start.11 = (s32[32]{0:T(128)S(1)}, s32[32]{0:T(128)S(1)}, u32[]{:S(2)}, u32[]{:S(2)}) collective-permute-start(s32[32]{0:T(128)S(1)} %collective-permute-done.7), channel_id=1, source_target_pairs={{0,7},{1,0},{2,1},{3,2},{4,3},{5,4},{6,5},{7,6},{8,15},{9,8},{10,9... | collective-permute-start | bytes 392 | tf_op jit(solution)/shard_map/ppermute | solution.py:12
  75.0 75.7 %collective-permute-start.13 = (bf16[32,128,128]{2,1,0:T(8,128)(2,1)}, bf16[32,128,128]{2,1,0:T(8,128)(2,1)}, u32[]{:S(2)}, u32[]{:S(2)}) collective-permute-start(bf16[32,128,128]{2,1,0:T(8,128)(2,1)} %collective-permute-done.9), channel_id=1, source_target_pairs={{0,24},{8,0},{16,8},{24,16},{1,25},{9,1},{17,9},{25,17},{2,26},{10... | collective-permute-start | bytes 3145736 | tf_op jit(solution)/shard_map/ppermute | solution.py:12
  76.2 74.5 %collective-permute-start.12 = (bf16[32,128,128]{2,1,0:T(8,128)(2,1)}, bf16[32,128,128]{2,1,0:T(8,128)(2,1)}, u32[]{:S(2)}, u32[]{:S(2)}) collective-permute-start(bf16[32,128,128]{2,1,0:T(8,128)(2,1)} %collective-permute-done.8), channel_id=1, source_target_pairs={{0,7},{1,0},{2,1},{3,2},{4,3},{5,4},{6,5},{7,6},{8,15},{9,8},{10,9... | collective-permute-start | bytes 3145736 | tf_op jit(solution)/shard_map/ppermute | solution.py:12
  184.4 52.8 %all-to-all-start.1 = ((bf16[64,128,128]{2,1,0:T(8,128)(2,1)}), bf16[64,128,128]{2,1,0:T(8,128)(2,1)S(1)}, u32[]{:S(2)}, u32[]{:S(2)}) async-start(bf16[64,128,128]{2,1,0:T(8,128)(2,1)} %scatter_fusion.4), calls=%async_computation.1 | async-start | bytes 4194304 | tf_op jit(solution)/shard_map/all_to_all | solution.py:82
where the time goes:
time: 250 us; the launch traced here: 248 us
  waiting for transfers between devices  84.8 us (34%)
  other arithmetic  61.7 us (25%)
  local copies, waits for them, and re-layouts  50 us (20%)
  starting transfers between devices  35.8 us (14%)
  matrix products  15.2 us (6%)
    scatter-add x4, other arithmetic, add_products(): accumulated.at[targets.reshape(-1)]  54.2 us
    all_to_all x1, waiting for transfers between devices, body(): lax.all_to_all(send_blocks, ('row', 'col'), split_axis=0, concat_axis=0,...  49.3 us
    ppermute x14, waiting for transfers between devices, passed_along(): lax.ppermute(shard, axis, [(i, (i + by) % devices) for i in range(devices)])  35.5 us
    ppermute x14, starting transfers between devices, passed_along(): lax.ppermute(shard, axis, [(i, (i + by) % devices) for i in range(devices)])  28.2 us
    transpose x4, local copies, waits for them, and re-layouts, add_products(): jnp.einsum('kaxy,kbyz->kabxz', left_blocks, right_blocks, preferred_eleme...  21.4 us
    dot_general x4, matrix products, add_products(): jnp.einsum('kaxy,kbyz->kabxz', left_blocks, right_blocks, preferred_eleme...  15.2 us
    scatter x1, local copies, waits for them, and re-layouts, body(): owned_blocks = owned_blocks.at[recv_slots].set(recv_blocks, mode='drop')  8.58 us
  transfers between devices with their start and end apart: 16, of which 5 were waited for; matrix products, arithmetic and copies ran while one was open for 47% of the time, Pallas kernels for 0%

commit v1 on v0

v1 whole, which is shorter than its diff:
```python
import functools

import jax
import jax.numpy as jnp
from jax import lax
from jax.experimental import pallas as pl
from jax.experimental.pallas import tpu as pltpu
from jax.sharding import PartitionSpec as P

RB = 8
SCAP = 2
UNROLL = 8
CORES = 2
SIDE = 2
PARTS = 2
EXCHANGE_ROWS = 8
LANES = 128

SMEM = pl.BlockSpec(memory_space=pltpu.SMEM)
VMEM = pl.BlockSpec(memory_space=pltpu.VMEM)
HBM = pl.BlockSpec(memory_space=pltpu.HBM)
ANY = pl.BlockSpec(memory_space=pl.ANY)


def limit(megabytes):
    return pltpu.CompilerParams(vmem_limit_bytes=megabytes * 1024 * 1024)


def announce_kernel(told, ids, out_ref, pos, base, sent):
    kept_count = pos.shape[0]
    base[...] = jnp.zeros_like(base)
    base[pl.ds(0, 1), :] = jnp.full((1, LANES), SCAP * out_ref.shape[0], jnp.int32)
    base[pl.ds(1, 1), pl.ds(0, ids.shape[1])] = ids[...]
    out_ref[...] = jnp.broadcast_to(base[...][None], out_ref.shape)
    lane = lax.broadcasted_iota(jnp.int32, (1, LANES), 1)

    def clear(d, carry):
        sent[d] = 0
        return carry

    lax.fori_loop(0, out_ref.shape[0], clear, 0, unroll=8)

    def tell(q, carry):
        owner = told[q]
        order = sent[owner]
        pos[q] = owner * SCAP + order
        sent[owner] = order + 1
        out_ref[owner, pl.ds(0, 1), :] = jnp.where(lane == order, told[kept_count + q], out_ref[owner, pl.ds(0, 1), :])
        return carry

    lax.fori_loop(0, kept_count, tell, 0)


def announce(device_count, owners, slots, a_ids, b_ids):
    return pl.pallas_call(
        announce_kernel,
        out_shape=[
            pltpu.VMEM((device_count, EXCHANGE_ROWS, LANES), jnp.int32),
            jax.ShapeDtypeStruct(owners.shape, jnp.int32),
        ],
        in_specs=[SMEM, VMEM],
        out_specs=[VMEM, SMEM],
        scratch_shapes=[pltpu.VMEM((EXCHANGE_ROWS, LANES), jnp.int32), pltpu.SMEM((device_count,), jnp.int32)],
        compiler_params=limit(2),
        name="announce",
    )(jnp.concatenate([owners, slots]), jnp.concatenate([a_ids, b_ids], axis=1))


def choose_kernel(cuts, where, *refs):
    count = len(cuts)
    pairs = [(refs[2 * n], refs[2 * n + 1]) for n in range(count)]
    out_refs, sems = list(refs[2 * count + 1:-1]), refs[-1]
    core = where[1] % CORES
    waits = []
    for (first, second), parts in zip(pairs, cuts):
        size = first.shape[0] // parts
        for part in range(parts):
            out, sem, rows = out_refs[len(waits)], sems.at[len(waits)], pl.ds(part * size, size)
            pl.when(core == 0)(pltpu.make_async_copy(first.at[rows], out, sem).start)
            pl.when(core != 0)(pltpu.make_async_copy(second.at[rows], out, sem).start)
            waits.append(pltpu.make_async_copy(first.at[rows], out, sem))
    for copy in waits:
        copy.wait()


def choose(where, pairs, cuts, after):
    shapes = [
        pltpu.VMEM((first.shape[0] // parts, first.shape[1]), first.dtype)
        for (first, _), parts in zip(pairs, cuts)
        for _ in range(parts)
    ]
    return pl.pallas_call(
        functools.partial(choose_kernel, cuts),
        out_shape=shapes,
        in_specs=[SMEM] + [ANY] * (2 * len(pairs) + 1),
        out_specs=[VMEM] * len(shapes),
        scratch_shapes=[pltpu.SemaphoreType.DMA((len(shapes),))],
        compiler_params=limit(8),
        name="choose",
    )(where, *(piece for pair in pairs for piece in pair), after)


def tie_kernel(*refs):
    pass


def tied(array, after):
    return pl.pallas_call(
        tie_kernel,
        out_shape=jax.ShapeDtypeStruct(array.shape, array.dtype),
        in_specs=[ANY] * 2,
        out_specs=ANY,
        input_output_aliases={0: 0},
        compiler_params=limit(1),
        name="tied",
    )(array, after)


class Bringer:
    def __init__(self, a_ref, b_ref, sems, row_count, col_count):
        self.refs = {"a": (a_ref, a_ref.shape[0] // row_count), "b": (b_ref, b_ref.shape[0] // col_count)}
        self.sems, self.copies = sems, []

    def bring(self, which, ref, member, part=0, parts=1):
        target, size = self.refs[which]
        size //= parts
        rows = target.at[pl.ds(pl.multiple_of((member * parts + part) * size, size), size)]
        self.copies.append(pltpu.make_async_copy(ref, rows, self.sems.at[len(self.copies)]))
        self.copies[-1].start()

    def wait(self):
        for copy in self.copies:
            copy.wait()


def bring_chip(bringer, refs, shift, j, chips, parts=1):
    z, core = j // CORES, j % CORES
    for ref_core in (core, CORES - 1 - core):
        for part in range(parts):
            bringer.bring("b", refs.pop(0), (z - shift + chips) % chips * CORES + ref_core, part, parts)


def bring_first(bringer, refs, i, j, row_count, col_count):
    refs = list(refs)
    y_count, chips = row_count // SIDE, col_count // CORES
    y, x = i // SIDE, i % SIDE
    bringer.bring("a", refs.pop(0), i)
    bringer.bring("a", refs.pop(0), y * SIDE + SIDE - 1 - x)
    for shift in range(1, y_count):
        bringer.bring("a", refs.pop(0), (y - shift + y_count) % y_count * SIDE + x)
    for shift in (0, 1, chips - 1):
        bring_chip(bringer, refs, shift, j, chips)


def bring_rest(bringer, refs, i, j, row_count, col_count):
    refs = list(refs)
    y_count, chips = row_count // SIDE, col_count // CORES
    y, x = i // SIDE, i % SIDE
    for shift in range(1, y_count):
        bringer.bring("a", refs.pop(0), (y - shift + y_count) % y_count * SIDE + SIDE - 1 - x)
    for shift in range(2, chips // 2):
        bring_chip(bringer, refs, shift, j, chips)
        bring_chip(bringer, refs, chips - shift, j, chips)
    bring_chip(bringer, refs, chips // 2, j, chips, PARTS)


class Layout:
    def __init__(self, row_count, col_count, b_slots, kept_count):
        self.count = 2 * col_count * b_slots + UNROLL
        self.i, self.j = self.count + 1, self.count + 2
        self.pos = self.count + 3
        self.source = self.pos + kept_count
        self.size = self.source + SCAP * row_count * col_count + 1


def multiply_listed(listed, count, a_ref, b_ref, total):
    block = a_ref.shape[-1]

    def block_of(ref, index):
        return ref[pl.ds(pl.multiple_of(index * block, block), block), :]

    def multiply(step, carry):
        entries = [listed[step * UNROLL + u] for u in range(UNROLL)]
        products = [
            jnp.dot(
                block_of(a_ref, (entry >> 10) & 1023),
                block_of(b_ref, entry & 1023),
                preferred_element_type=jnp.float32,
            )
            for entry in entries
        ]
        for entry, product in zip(entries, products):
            q = entry >> 20
            total[q] = total[q] + product
        return carry

    lax.fori_loop(0, (count + UNROLL - 1) // UNROLL, multiply, 0)


def first_kernel(sizes, parts, keep, pos, where, exchange, *refs):
    row_count, col_count, b_slots = sizes
    pieces, refs = refs[:parts], refs[parts:]
    a_ref, b_ref, total, plan, ids, places, table, slot_rows, slot_table, listed, sems, sem = refs
    i, j = where[0], where[1]
    kept_count = keep.shape[0]
    panel_width = RB * col_count // row_count
    chips = col_count // CORES
    capacity = SCAP * row_count * col_count
    layout = Layout(row_count, col_count, b_slots, kept_count)
    bringer = Bringer(a_ref, b_ref, sems, row_count, col_count)
    bring_first(bringer, pieces, i, j, row_count, col_count)

    slot_rows[...] = exchange[:, 0, :]
    to_slot_table = pltpu.make_async_copy(slot_rows, slot_table, sem.at[0])
    to_slot_table.start()

    halves = col_count // row_count
    for half_panel in range(col_count):
        member, half = half_panel // halves, half_panel % halves
        rows = exchange[member * col_count + j, pl.ds(1, 1), :]
        ids[pl.ds(half_panel, 1), :] = rows if half == 0 else pltpu.roll(rows, LANES - half * b_slots, 1)
        source = half * row_count + (member + j - i + row_count) % row_count
        cols = exchange[i * col_count + source, pl.ds(1, 1), :]
        ids[pl.ds(col_count + half_panel, 1), :] = pltpu.roll(cols, LANES - halves * b_slots, 1)
    rows = ids[pl.ds(0, col_count), :] * panel_width
    cols = ids[pl.ds(col_count, col_count), :]
    even = lax.broadcasted_iota(jnp.int32, cols.shape, 1) % 2 == 0
    crossed = jnp.where(even, pltpu.roll(cols, LANES - 1, 1), pltpu.roll(cols, 1, 1))
    for cross, columns in enumerate([cols, crossed]):
        target = rows + columns
        found = jnp.full_like(target, kept_count)
        for q in range(kept_count):
            found = jnp.where(target == keep[q], q, found)
        places[pl.ds(cross * col_count, col_count), :] = found
    to_table = pltpu.make_async_copy(places, table, sem.at[1])
    to_table.start()
    total[...] = jnp.zeros_like(total)
    to_table.wait()

    def look(half_panel, counts):
        member = half_panel // halves
        source = (half_panel % halves) * row_count + (member + j - i + row_count) % row_count
        a_near = (member % SIDE == i % SIDE) | (member // SIDE == i // SIDE)
        apart = jnp.abs(j // CORES - source // CORES)
        b_near = (apart <= 1) | (apart == chips - 1)

        def scan(into, n):
            for slot in range(b_slots):
                for cross in range(2):
                    q = table[cross * col_count + half_panel, slot]
                    into[n] = (q << 20) | ((half_panel * b_slots + slot) << 10) | (source * b_slots + (slot ^ cross))
                    n = n + (q < kept_count).astype(jnp.int32)
            return n

        return lax.cond(
            a_near & b_near,
            lambda near, far: (scan(listed, near), far),
            lambda near, far: (near, scan(plan, far)),
            *counts,
        )

    near, far = lax.fori_loop(0, col_count, look, (jnp.int32(0), jnp.int32(0)))
    for extra in range(UNROLL):
        listed[near + extra] = kept_count << 20
        plan[far + extra] = kept_count << 20
    plan[layout.count], plan[layout.i], plan[layout.j] = far, i, j
    for q in range(kept_count):
        plan[layout.pos + q] = pos[q]

    def clear(s, carry):
        plan[layout.source + s] = -1
        return carry

    lax.fori_loop(0, capacity + 1, clear, 0, unroll=5)
    to_slot_table.wait()

    def mark(d, carry):
        for m in range(SCAP):
            plan[layout.source + slot_table[d, m]] = d * SCAP + m
        return carry

    lax.fori_loop(0, row_count * col_count, mark, 0, unroll=8)
    bringer.wait()
    multiply_listed(listed, near, a_ref, b_ref, total)


def first_products(sizes, keep, pos, where, exchange, pieces):
    row_count, col_count, b_slots = sizes
    block, kept_count = pieces[0].shape[-1], keep.shape[0]
    rows = col_count * b_slots * block
    return pl.pallas_call(
        functools.partial(first_kernel, sizes, len(pieces)),
        out_shape=[
            pltpu.VMEM((rows, block), jnp.bfloat16),
            pltpu.VMEM((rows, block), jnp.bfloat16),
            pltpu.VMEM((kept_count + 1, block, block), jnp.float32),
            jax.ShapeDtypeStruct((Layout(row_count, col_count, b_slots, kept_count).size,), jnp.int32),
        ],
        in_specs=[SMEM] * 3 + [VMEM] + [ANY] * len(pieces),
        out_specs=[VMEM] * 3 + [SMEM],
        scratch_shapes=[
            pltpu.VMEM((2 * col_count, LANES), jnp.int32),
            pltpu.VMEM((2 * col_count, LANES), jnp.int32),
            pltpu.SMEM((2 * col_count, LANES), jnp.int32),
            pltpu.VMEM((row_count * col_count, LANES), jnp.int32),
            pltpu.SMEM((row_count * col_count, LANES), jnp.int32),
            pltpu.SMEM((2 * col_count * b_slots + UNROLL,), jnp.int32),
            pltpu.SemaphoreType.DMA((len(pieces),)),
            pltpu.SemaphoreType.DMA((2,)),
        ],
        compiler_params=limit(26),
        cost_estimate=pl.CostEstimate(flops=5 * 10**9, bytes_accessed=0, transcendentals=0),
        name="first_products",
    )(keep, pos, where, exchange, *pieces)


def rest_kernel(sizes, parts, plan, *refs):
    row_count, col_count, b_slots = sizes
    pieces, refs = refs[3:3 + parts], refs[3 + parts:]
    a_ref, b_ref, total, send_ref, kept, sems, sem = refs
    kept_count = kept.shape[0]
    layout = Layout(row_count, col_count, b_slots, kept_count)
    bringer = Bringer(a_ref, b_ref, sems, row_count, col_count)
    bring_rest(bringer, pieces, plan[layout.i], plan[layout.j], row_count, col_count)
    bringer.wait()
    multiply_listed(plan, plan[layout.count], a_ref, b_ref, total)

    def finish(q, carry):
        kept[q] = total[q].astype(jnp.bfloat16)
        pltpu.make_async_copy(kept.at[q], send_ref.at[plan[layout.pos + q]], sem).start()
        return carry

    lax.fori_loop(0, kept_count, finish, 0, unroll=2)
    pltpu.make_async_copy(kept, kept, sem).wait()


def rest_products(sizes, kept_count, plan, buffers, pieces):
    row_count, col_count = sizes[:2]
    block = pieces[0].shape[-1]
    return pl.pallas_call(
        functools.partial(rest_kernel, sizes, len(pieces)),
        out_shape=[pltpu.VMEM(b.shape, b.dtype) for b in buffers]
        + [pltpu.HBM((SCAP * row_count * col_count, block, block), jnp.bfloat16)],
        in_specs=[SMEM] + [VMEM] * 3 + [ANY] * len(pieces),
        out_specs=[VMEM] * 3 + [HBM],
        scratch_shapes=[
            pltpu.VMEM((kept_count, block, block), jnp.bfloat16),
            pltpu.SemaphoreType.DMA((len(pieces),)),
            pltpu.SemaphoreType.DMA,
        ],
        input_output_aliases={1 + n: n for n in range(3)},
        compiler_params=limit(28),
        name="rest_products",
    )(plan, *buffers, *pieces)[-1]


def place_kernel(layout, plan, recv_ref, out_ref, zero, sem):
    zero[...] = jnp.zeros_like(zero)

    def place(s, carry):
        r = plan[layout.source + s]

        @pl.when(r >= 0)
        def _():
            pltpu.make_async_copy(recv_ref.at[r], out_ref.at[s], sem).start()

        @pl.when(r < 0)
        def _():
            pltpu.make_async_copy(zero, out_ref.at[s], sem).start()

        return carry

    lax.fori_loop(0, out_ref.shape[0], place, 0, unroll=4)
    pltpu.make_async_copy(recv_ref, out_ref, sem).wait()


def place(layout, plan, recv):
    block = recv.shape[-1]
    return pl.pallas_call(
        functools.partial(place_kernel, layout),
        out_shape=jax.ShapeDtypeStruct(recv.shape, recv.dtype),
        in_specs=[SMEM, VMEM],
        out_specs=HBM,
        scratch_shapes=[pltpu.VMEM((block, block), jnp.bfloat16), pltpu.SemaphoreType.DMA],
        compiler_params=limit(12),
        name="place",
    )(plan, recv)


def gathered(a_own, b_own, row_count, col_count, where, outgoing, multiply_near):
    chips, shifts = col_count // CORES, range(1, row_count // SIDE)

    def moved(piece, target):
        pairs = [(d, c, target(d, c)) for d in range(row_count) for c in range(col_count)]
        return lax.ppermute(
            piece, ("row", "col"), [(d * col_count + c, to[0] * col_count + to[1]) for d, c, to in pairs]
        )

    def around(d, c, by, other=False):
        core = CORES - 1 - c % CORES if other else c % CORES
        return d, (c // CORES + by) % chips * CORES + core

    def along(d, c, shift):
        return (d + shift * SIDE) % row_count, c

    def swapped(piece):
        return moved(piece, lambda d, c: around(d, c, 0, True))

    below = [moved(b_own, lambda d, c: around(d, c, 1))]
    above = [moved(b_own, lambda d, c: around(d, c, -1))]
    beside = moved(a_own, lambda d, c: (d ^ 1, c))
    ahead = [moved(a_own, lambda d, c, shift=shift: along(d, c, shift)) for shift in shifts]
    exchange = lax.all_to_all(outgoing, ("row", "col"), split_axis=0, concat_axis=0, tiled=True)
    for _ in range(2, chips // 2):
        below.append(moved(below[-1], lambda d, c: around(d, c, 1)))
        above.append(moved(above[-1], lambda d, c: around(d, c, -1)))
    pairs = [(below[-1], above[-1])] + [(piece, beside) for piece in ahead]
    cuts = [PARTS] + [1] * len(ahead)
    chosen = choose(where, pairs, cuts, exchange)
    passed, crossing = chosen[:PARTS], chosen[PARTS:]
    opposite = [moved(part, lambda d, c: around(d, c, 1 if c % CORES == 0 else -1)) for part in passed]
    diagonal = [
        moved(piece, lambda d, c, shift=shift: (d ^ 1, c) if c % CORES == 0 else along(d, c, shift))
        for shift, piece in zip(shifts, crossing)
    ]

    near = [a_own, beside, *ahead]
    for piece in (b_own, below[0], above[0]):
        near += [piece, swapped(piece)]
    *buffers, plan = multiply_near(exchange, near)
    opposite[-1] = tied(opposite[-1], plan)
    far = list(diagonal)
    for n in range(1, chips // 2 - 1):
        far += [below[n], swapped(below[n]), above[n], swapped(above[n])]
    return buffers, plan, far + opposite + [swapped(part) for part in opposite]


def body(a_blocks, a_rows, b_blocks, b_cols, c_keep, c_owner, c_slot):
    row_count = lax.axis_size("row")
    col_count = lax.axis_size("col")
    device_count = row_count * col_count
    block = a_blocks.shape[-1]
    keep, owner_ids, slot_ids = c_keep[0, 0], c_owner[0, 0], c_slot[0, 0]
    sizes = (row_count, col_count, b_cols.shape[1])
    where = jnp.stack([lax.axis_index("row"), lax.axis_index("col")]).astype(jnp.int32)

    outgoing, pos = announce(device_count, owner_ids, slot_ids, a_rows, b_cols)

    buffers, plan, far = gathered(
        a_blocks[0].reshape(-1, block),
        b_blocks[0].reshape(-1, block),
        row_count,
        col_count,
        where,
        outgoing,
        functools.partial(first_products, sizes, keep, pos, where),
    )
    send = rest_products(sizes, keep.shape[0], plan, buffers, far)
    recv = lax.all_to_all(send, ("row", "col"), split_axis=0, concat_axis=0, tiled=True)
    return place(Layout(*sizes, keep.shape[0]), plan, recv)[None]


def solution(mesh):
    return jax.shard_map(
        body,
        mesh=mesh,
        in_specs=(
            P("col", "row", None, None),
            P("col", "row"),
            P("row", "col", None, None),
            P("row", "col"),
            P("row", "col", None),
            P("row", "col", None),
            P("row", "col", None),
        ),
        out_specs=P("row", "col", None, None),
        check_vma=False,
    )
```

time: 250 us -> 110 us (0.44)
  other arithmetic: 61.7 us -> 1.57 us
  waiting for transfers between devices: 84.8 us -> 26.7 us
  blocking collectives: 0 us -> 53.5 us
  local copies, waits for them, and re-layouts: 50 us -> 0.01 us
  starting transfers between devices: 35.8 us -> 16.7 us
  matrix products: 15.2 us -> 0 us
  Pallas kernels: 0 us -> 11.4 us
    scatter-add x4 -> x0, other arithmetic: 54.2 us -> none  [add_products(): accumulated.at[targets.reshape(-1)]]
    all_to_all x0 -> x1, blocking collectives: none -> 53.5 us  [body(): lax.all_to_all(send, ('row', 'col'), split_axis=0, concat_axis=0, tiled=T...]
    all_to_all x2 -> x1, waiting for transfers between devices: 49.3 us -> 0.95 us  [gathered(): lax.all_to_all(outgoing, ('row', 'col'), split_axis=0, concat_axis=0, til...]
    transpose x4 -> x0, local copies, waits for them, and re-layouts: 21.4 us -> none  [add_products(): jnp.einsum('kaxy,kbyz->kabxz', left_blocks, right_blocks, preferred_eleme...]
    ppermute x14 -> x12, starting transfers between devices: 28.2 us -> 12.5 us  [moved(): lax.ppermute(piece, ('row', 'col'), [(d * col_count + c, to[0] * col_coun...]
    dot_general x4 -> x0, matrix products: 15.2 us -> none  [add_products(): jnp.einsum('kaxy,kbyz->kabxz', left_blocks, right_blocks, preferred_eleme...]
    scatter x3 -> x0, local copies, waits for them, and re-layouts: 13.9 us -> none  [the longest x1 8.58 us: body(): owned_blocks = owned_blocks.at[recv_slots].set(recv_blocks, mode='drop')]
    pallas_call x0 -> x6, Pallas kernels: none -> 11.4 us  [the longest x1 5.01 us: first_products(): pl.pallas_call(functools.partial(first_kernel, sizes, len(pieces)), out_s...]
  transfers between devices with their start and end apart: 16 -> 13, of which waited for: 5 -> 6; matrix products, arithmetic and copies ran while one was open for 47% -> 1% of each run, Pallas kernels for 0% -> 7%
where the time goes in v1:
time: 110 us
  blocking collectives  53.5 us (49%)
  waiting for transfers between devices  26.7 us (24%)
  starting transfers between devices  16.7 us (15%)
  Pallas kernels  11.4 us (10%)
  other arithmetic  1.57 us (1%)
    all_to_all x1, blocking collectives, body(): lax.all_to_all(send, ('row', 'col'), split_axis=0, concat_axis=0, tiled=T...  53.5 us
    ppermute x12, waiting for transfers between devices, moved(): lax.ppermute(piece, ('row', 'col'), [(d * col_count + c, to[0] * col_coun...  25.7 us
    ppermute x12, starting transfers between devices, moved(): lax.ppermute(piece, ('row', 'col'), [(d * col_count + c, to[0] * col_coun...  12.5 us
    pallas_call x1, Pallas kernels, first_products(): pl.pallas_call(functools.partial(first_kernel, sizes, len(pieces)), out_s...  5.01 us
    all_to_all x1, starting transfers between devices, gathered(): lax.all_to_all(outgoing, ('row', 'col'), split_axis=0, concat_axis=0, til...  4.19 us
    pallas_call x1, Pallas kernels, rest_products(): pl.pallas_call(functools.partial(rest_kernel, sizes, len(pieces)), out_sh...  2.38 us
  transfers between devices with their start and end apart: 13, of which 6 were waited for; matrix products, arithmetic and copies ran while one was open for 1% of the time, Pallas kernels for 7%

profile of v1, /device:TPU:0, one launch (start us, length us, event | category | flops | bytes accessed | tf_op | source)
XLA Modules:
  0.0 110.0 jit_solution(16459938667355481261)
XLA Ops:
  0.0 3.0 %collective-permute-start.1 = (bf16[4096,128]{1,0:T(8,128)(2,1)}, bf16[4096,128]{1,0:T(8,128)(2,1)S(1)}, u32[]{:S(2)}, u32[]{:S(2)}) collective-permute-start(bf16[4096,128]{1,0:T(8,128)(2,1)} %bitcast.8), channel_id=1, source_target_pairs={{0,16},{1,17},{2,18},{3,19},{4,20},{5,21},{6,22},{7,23},{8,24},{9,... | collective-permute-start | bytes 3145736 | tf_op jit(solution)/shard_map/ppermute | solution.py:395
  3.0 1.5 %collective-permute-start = (bf16[4096,128]{1,0:T(8,128)(2,1)}, bf16[4096,128]{1,0:T(8,128)(2,1)S(1)}, u32[]{:S(2)}, u32[]{:S(2)}) collective-permute-start(bf16[4096,128]{1,0:T(8,128)(2,1)} %bitcast.9), channel_id=1, source_target_pairs={{0,8},{1,9},{2,10},{3,11},{4,12},{5,13},{6,14},{7,15},{8,0},{9,1},... | collective-permute-start | bytes 3145736 | tf_op jit(solution)/shard_map/ppermute | solution.py:395
  4.5 3.6 %collective-permute-start.5 = (bf16[2048,128]{1,0:T(8,128)(2,1)}, bf16[2048,128]{1,0:T(8,128)(2,1)S(1)}, u32[]{:S(2)}, u32[]{:S(2)}) collective-permute-start(bf16[2048,128]{1,0:T(8,128)(2,1)} %bitcast.11), channel_id=1, source_target_pairs={{0,6},{1,7},{2,0},{3,1},{4,2},{5,3},{6,4},{7,5},{8,14},{9,15},{10,... | collective-permute-start | bytes 1572872 | tf_op jit(solution)/shard_map/ppermute | solution.py:395
  8.1 0.0 collective-permute-start.3
  8.1 0.7 pad_add_fusion.1.ids
  8.8 0.7 pad_add_fusion.told
  9.6 1.5 %announce.1 = (s32[32,8,128]{2,1,0:T(8,128)}, s32[24]{0:T(128)S(1)}) custom-call(s32[48]{0:T(128)S(1)} %pad_add_fusion.told, s32[1,48]{1,0:T(1,128)S(1)} %pad_add_fusion.1.ids), custom_call_target="tpu_custom_call" | custom-call | tf_op jit(solution)/shard_map/announce/pallas_call | solution.py:55
  11.0 4.2 %all-to-all-start = ((s32[32,8,128]{2,1,0:T(8,128)}), s32[32,8,128]{2,1,0:T(8,128)S(1)}, u32[]{:S(2)}, u32[]{:S(2)}) async-start(s32[32,8,128]{2,1,0:T(8,128)} %get-tuple-element.16), calls=%async_computation | async-start | bytes 262144 | tf_op jit(solution)/shard_map/all_to_all | solution.py:413
  15.2 0.3 collective-permute-start.2
  15.6 5.2 %collective-permute-done.5.refs_7_.refs_1_ = bf16[2048,128]{1,0:T(8,128)(2,1)S(1)} collective-permute-done((bf16[2048,128]{1,0:T(8,128)(2,1)}, bf16[2048,128]{1,0:T(8,128)(2,1)S(1)}, u32[]{:S(2)}, u32[]{:S(2)}) %collective-permute-start.5) | collective-permute-done | bytes 524320 | tf_op jit(solution)/shard_map/ppermute | solution.py:395
  20.8 11.4 %collective-permute-done.3.refs_5_.refs_0_ = bf16[2048,128]{1,0:T(8,128)(2,1)S(1)} collective-permute-done((bf16[2048,128]{1,0:T(8,128)(2,1)}, bf16[2048,128]{1,0:T(8,128)(2,1)S(1)}, u32[]{:S(2)}, u32[]{:S(2)}) %collective-permute-start.3) | collective-permute-done | bytes 524320 | tf_op jit(solution)/shard_map/ppermute | solution.py:395
  32.1 0.1 pad_add_fusion.2.where
  32.2 0.9 all-to-all-done.exchange.refs_4_
  33.2 0.7 choose.1
  33.9 1.3 %collective-permute-start.7 = (bf16[4096,128]{1,0:T(8,128)(2,1)S(1)}, bf16[4096,128]{1,0:T(8,128)(2,1)S(1)}, u32[]{:S(2)}, u32[]{:S(2)}) collective-permute-start(bf16[4096,128]{1,0:T(8,128)(2,1)S(1)} %get-tuple-element.21), channel_id=1, source_target_pairs={{0,8},{1,17},{2,10},{3,19},{4,12},{5,21},{6,14},{7,23},{8,0},{9,25... | collective-permute-start | bytes 3145736 | tf_op jit(solution)/shard_map/ppermute | solution.py:395
  35.2 1.7 %collective-permute-start.8 = (bf16[1024,128]{1,0:T(8,128)(2,1)S(1)}, bf16[1024,128]{1,0:T(8,128)(2,1)S(1)}, u32[]{:S(2)}, u32[]{:S(2)}) collective-permute-start(bf16[1024,128]{1,0:T(8,128)(2,1)S(1)} %get-tuple-element.22), channel_id=1, source_target_pairs={{0,2},{1,7},{2,4},{3,1},{4,6},{5,3},{6,0},{7,5},{8,10},{9,15},{10,... | collective-permute-start | bytes 786440 | tf_op jit(solution)/shard_map/ppermute | solution.py:395
  36.9 1.2 %collective-permute-start.9 = (bf16[1024,128]{1,0:T(8,128)(2,1)S(1)}, bf16[1024,128]{1,0:T(8,128)(2,1)S(1)}, u32[]{:S(2)}, u32[]{:S(2)}) collective-permute-start(bf16[1024,128]{1,0:T(8,128)(2,1)S(1)} %get-tuple-element.23), channel_id=1, source_target_pairs={{0,2},{1,7},{2,4},{3,1},{4,6},{5,3},{6,0},{7,5},{8,10},{9,15},{10,... | collective-permute-start | bytes 786440 | tf_op jit(solution)/shard_map/ppermute | solution.py:395
  38.1 5.0 %first_products.1 = (bf16[16384,128]{1,0:T(8,128)(2,1)S(1)}, bf16[16384,128]{1,0:T(8,128)(2,1)S(1)}, f32[25,128,128]{2,1,0:T(8,128)S(1)}, s32[356]{0:T(512)S(1)}) custom-call(s32[24]{0:T(128)S(1)} %bitcast.15, s32[24]{0:T(128)S(1)} %get-tuple-element.15.pos, s32[2]{0:T(128)S(1)} %pad_add_fusion.2.where, s32[32,8,128]{2,1,0:T(8,128)S(1)} %all-to-all-done.exchange.refs_4_, ...), custom_call_target="tpu_custom_call" | custom-call | flops 5000000000 | tf_op jit(solution)/shard_map/first_products/pallas_call | solution.py:291
  43.1 3.1 %collective-permute-done.8.refs_4_ = bf16[1024,128]{1,0:T(8,128)(2,1)S(1)} collective-permute-done((bf16[1024,128]{1,0:T(8,128)(2,1)S(1)}, bf16[1024,128]{1,0:T(8,128)(2,1)S(1)}, u32[]{:S(2)}, u32[]{:S(2)}) %collective-permute-start.8) | collective-permute-done | bytes 262176 | tf_op jit(solution)/shard_map/ppermute | solution.py:395
  46.2 4.5 %collective-permute-done.9.refs_0_ = bf16[1024,128]{1,0:T(8,128)(2,1)S(1)} collective-permute-done((bf16[1024,128]{1,0:T(8,128)(2,1)S(1)}, bf16[1024,128]{1,0:T(8,128)(2,1)S(1)}, u32[]{:S(2)}, u32[]{:S(2)}) %collective-permute-start.9) | collective-permute-done | bytes 262176 | tf_op jit(solution)/shard_map/ppermute | solution.py:395
  50.7 1.5 %collective-permute-done.11.refs_7_ = bf16[1024,128]{1,0:T(8,128)(2,1)S(1)} collective-permute-done((bf16[1024,128]{1,0:T(8,128)(2,1)S(1)}, bf16[1024,128]{1,0:T(8,128)(2,1)S(1)}, u32[]{:S(2)}, u32[]{:S(2)}) %collective-permute-start.11) | collective-permute-done | bytes 262176 | tf_op jit(solution)/shard_map/ppermute | solution.py:395
  52.2 2.4 %rest_products.1 = (bf16[16384,128]{1,0:T(8,128)(2,1)S(1)}, bf16[16384,128]{1,0:T(8,128)(2,1)S(1)}, f32[25,128,128]{2,1,0:T(8,128)S(1)}, bf16[64,128,128]{2,1,0:T(8,128)(2,1)}) custom-call(s32[356]{0:T(512)S(1)} %get-tuple-element.17.refs_1_.plan, ...), custom_call_target="tpu_custom_call", output_to_operand_aliasing={{0}: (1, {}), {1}: (2, {}), {2}: (3, {})} | custom-call | tf_op jit(solution)/shard_map/rest_products/pallas_call | solution.py:340
  54.6 53.5 %all_to_all.10.recv_ref = bf16[64,128,128]{2,1,0:T(8,128)(2,1)S(1)} all-to-all(bf16[64,128,128]{2,1,0:T(8,128)(2,1)} %get-tuple-element.24), channel_id=1, replica_groups=mesh['row'=4,'col'=8] {'row','col'}, dimensions={0} | all-to-all | bytes 4194304 | tf_op jit(solution)/shard_map/all_to_all | solution.py:459
  108.2 1.9 %place.1 = bf16[64,128,128]{2,1,0:T(8,128)(2,1)} custom-call(s32[356]{0:T(512)S(1)} %get-tuple-element.17.refs_1_.plan, bf16[64,128,128]{2,1,0:T(8,128)(2,1)S(1)} %all_to_all.10.recv_ref), custom_call_target="tpu_custom_call" | custom-call | tf_op jit(solution)/shard_map/place/pallas_call | solution.py:379
  (18 shorter events, 0.0 us)
Async XLA Ops:
  0.0 38.0 %copy-start.2 = (s32[1,1,24]{2,1,0:T(1,128)S(1)}, s32[1,1,24]{2,1,0:T(1,128)}, u32[]{:S(2)}) copy-start(s32[1,1,24]{2,1,0:T(1,128)} %param.11) | copy-start | bytes 292
  0.0 33.2 %collective-permute-start.1 = (bf16[4096,128]{1,0:T(8,128)(2,1)}, bf16[4096,128]{1,0:T(8,128)(2,1)S(1)}, u32[]{:S(2)}, u32[]{:S(2)}) collective-permute-start(bf16[4096,128]{1,0:T(8,128)(2,1)} %bitcast.8), channel_id=1, source_target_pairs={{0,16},{1,17},{2,18},{3,19},{4,20},{5,21},{6,22},{7,23},{8,24},{9,... | collective-permute-start | bytes 3145736 | tf_op jit(solution)/shard_map/ppermute | solution.py:395
  3.0 30.2 %collective-permute-start = (bf16[4096,128]{1,0:T(8,128)(2,1)}, bf16[4096,128]{1,0:T(8,128)(2,1)S(1)}, u32[]{:S(2)}, u32[]{:S(2)}) collective-permute-start(bf16[4096,128]{1,0:T(8,128)(2,1)} %bitcast.9), channel_id=1, source_target_pairs={{0,8},{1,9},{2,10},{3,11},{4,12},{5,13},{6,14},{7,15},{8,0},{9,1},... | collective-permute-start | bytes 3145736 | tf_op jit(solution)/shard_map/ppermute | solution.py:395
  4.5 16.3 %collective-permute-start.5 = (bf16[2048,128]{1,0:T(8,128)(2,1)}, bf16[2048,128]{1,0:T(8,128)(2,1)S(1)}, u32[]{:S(2)}, u32[]{:S(2)}) collective-permute-start(bf16[2048,128]{1,0:T(8,128)(2,1)} %bitcast.11), channel_id=1, source_target_pairs={{0,6},{1,7},{2,0},{3,1},{4,2},{5,3},{6,4},{7,5},{8,14},{9,15},{10,... | collective-permute-start | bytes 1572872 | tf_op jit(solution)/shard_map/ppermute | solution.py:395
  8.1 24.1 %collective-permute-start.3 = (bf16[2048,128]{1,0:T(8,128)(2,1)}, bf16[2048,128]{1,0:T(8,128)(2,1)S(1)}, u32[]{:S(2)}, u32[]{:S(2)}) collective-permute-start(bf16[2048,128]{1,0:T(8,128)(2,1)} %bitcast.12), channel_id=1, source_target_pairs={{0,2},{1,3},{2,4},{3,5},{4,6},{5,7},{6,0},{7,1},{8,10},{9,11},{10,... | collective-permute-start | bytes 1572872 | tf_op jit(solution)/shard_map/ppermute | solution.py:395
  11.0 22.1 %all-to-all-start = ((s32[32,8,128]{2,1,0:T(8,128)}), s32[32,8,128]{2,1,0:T(8,128)S(1)}, u32[]{:S(2)}, u32[]{:S(2)}) async-start(s32[32,8,128]{2,1,0:T(8,128)} %get-tuple-element.16), calls=%async_computation | async-start | bytes 262144 | tf_op jit(solution)/shard_map/all_to_all | solution.py:413
  15.2 21.6 %collective-permute-start.2 = (bf16[2048,128]{1,0:T(8,128)(2,1)}, bf16[2048,128]{1,0:T(8,128)(2,1)}, u32[]{:S(2)}, u32[]{:S(2)}) collective-permute-start(bf16[2048,128]{1,0:T(8,128)(2,1)} %bitcast.13), channel_id=1, source_target_pairs={{0,1},{1,0},{2,3},{3,2},{4,5},{5,4},{6,7},{7,6},{8,9},{9,8},{10,11... | collective-permute-start | bytes 1572872 | tf_op jit(solution)/shard_map/ppermute | solution.py:395
  20.8 17.3 %collective-permute-start.6 = (bf16[2048,128]{1,0:T(8,128)(2,1)S(1)}, bf16[2048,128]{1,0:T(8,128)(2,1)}, u32[]{:S(2)}, u32[]{:S(2)}) collective-permute-start(bf16[2048,128]{1,0:T(8,128)(2,1)S(1)} %collective-permute-done.5.refs_7_.refs_1_), channel_id=1, source_target_pairs={{0,1},{1,0},{2,3},{3,2},{4,5},{5,4},{6,7},{7,6},{8,9},{9,8},{10,11... | collective-permute-start | bytes 1572872 | tf_op jit(solution)/shard_map/ppermute | solution.py:395
  32.1 5.9 %collective-permute-start.4 = (bf16[2048,128]{1,0:T(8,128)(2,1)S(1)}, bf16[2048,128]{1,0:T(8,128)(2,1)}, u32[]{:S(2)}, u32[]{:S(2)}) collective-permute-start(bf16[2048,128]{1,0:T(8,128)(2,1)S(1)} %collective-permute-done.3.refs_5_.refs_0_), channel_id=1, source_target_pairs={{0,1},{1,0},{2,3},{3,2},{4,5},{5,4},{6,7},{7,6},{8,9},{9,8},{10,11... | collective-permute-start | bytes 1572872 | tf_op jit(solution)/shard_map/ppermute | solution.py:395
  33.2 4.9 %copy-start = (bf16[1,32,128,128]{3,2,1,0:T(8,128)(2,1)S(1)}, bf16[1,32,128,128]{3,2,1,0:T(8,128)(2,1)}, u32[]{:S(2)}) copy-start(bf16[1,32,128,128]{3,2,1,0:T(8,128)(2,1)} %param.7) | copy-start | bytes 3145732
  33.2 4.9 %copy-start.1 = (bf16[1,16,128,128]{3,2,1,0:T(8,128)(2,1)S(1)}, bf16[1,16,128,128]{3,2,1,0:T(8,128)(2,1)}, u32[]{:S(2)}) copy-start(bf16[1,16,128,128]{3,2,1,0:T(8,128)(2,1)} %param.9) | copy-start | bytes 1572868
  33.9 18.3 %collective-permute-start.7 = (bf16[4096,128]{1,0:T(8,128)(2,1)S(1)}, bf16[4096,128]{1,0:T(8,128)(2,1)S(1)}, u32[]{:S(2)}, u32[]{:S(2)}) collective-permute-start(bf16[4096,128]{1,0:T(8,128)(2,1)S(1)} %get-tuple-element.21), channel_id=1, source_target_pairs={{0,8},{1,17},{2,10},{3,19},{4,12},{5,21},{6,14},{7,23},{8,0},{9,25... | collective-permute-start | bytes 3145736 | tf_op jit(solution)/shard_map/ppermute | solution.py:395
  35.2 11.0 %collective-permute-start.8 = (bf16[1024,128]{1,0:T(8,128)(2,1)S(1)}, bf16[1024,128]{1,0:T(8,128)(2,1)S(1)}, u32[]{:S(2)}, u32[]{:S(2)}) collective-permute-start(bf16[1024,128]{1,0:T(8,128)(2,1)S(1)} %get-tuple-element.22), channel_id=1, source_target_pairs={{0,2},{1,7},{2,4},{3,1},{4,6},{5,3},{6,0},{7,5},{8,10},{9,15},{10,... | collective-permute-start | bytes 786440 | tf_op jit(solution)/shard_map/ppermute | solution.py:395
  36.9 13.8 %collective-permute-start.9 = (bf16[1024,128]{1,0:T(8,128)(2,1)S(1)}, bf16[1024,128]{1,0:T(8,128)(2,1)S(1)}, u32[]{:S(2)}, u32[]{:S(2)}) collective-permute-start(bf16[1024,128]{1,0:T(8,128)(2,1)S(1)} %get-tuple-element.23), channel_id=1, source_target_pairs={{0,2},{1,7},{2,4},{3,1},{4,6},{5,3},{6,0},{7,5},{8,10},{9,15},{10,... | collective-permute-start | bytes 786440 | tf_op jit(solution)/shard_map/ppermute | solution.py:395
  46.2 4.5 %collective-permute-start.10 = (bf16[1024,128]{1,0:T(8,128)(2,1)S(1)}, bf16[1024,128]{1,0:T(8,128)(2,1)S(1)}, u32[]{:S(2)}, u32[]{:S(2)}) collective-permute-start(bf16[1024,128]{1,0:T(8,128)(2,1)S(1)} %collective-permute-done.8.refs_4_), channel_id=1, source_target_pairs={{0,1},{1,0},{2,3},{3,2},{4,5},{5,4},{6,7},{7,6},{8,9},{9,8},{10,11... | collective-permute-start | bytes 786440 | tf_op jit(solution)/shard_map/ppermute | solution.py:395
  50.7 1.5 %collective-permute-start.11 = (bf16[1024,128]{1,0:T(8,128)(2,1)S(1)}, bf16[1024,128]{1,0:T(8,128)(2,1)S(1)}, u32[]{:S(2)}, u32[]{:S(2)}) collective-permute-start(bf16[1024,128]{1,0:T(8,128)(2,1)S(1)} %tied.1.refs_5_), channel_id=1, source_target_pairs={{0,1},{1,0},{2,3},{3,2},{4,5},{5,4},{6,7},{7,6},{8,9},{9,8},{10,11... | collective-permute-start | bytes 786440 | tf_op jit(solution)/shard_map/ppermute | solution.py:395

commit v2 on v1

--- a/solution.py
+++ b/solution.py
@@ -26,11 +26,25 @@
     return pltpu.CompilerParams(vmem_limit_bytes=megabytes * 1024 * 1024)
 
 
-def announce_kernel(told, ids, out_ref, pos, base, sent):
+def by_column(device, row_count, col_count):
+    return device % col_count * row_count + device // col_count
+
+
+def announce_kernel(
+    row_count, col_count, owners_ref, slots_ref, a_ids_ref, b_ids_ref, out_ref, pos,
+    base, sent, owners, slots, a_ids, b_ids, sems,
+):
+    moves = [(owners_ref, owners), (slots_ref, slots), (a_ids_ref, a_ids), (b_ids_ref, b_ids)]
+    copies = [pltpu.make_async_copy(source, target, sems.at[n]) for n, (source, target) in enumerate(moves)]
+    for copy in copies:
+        copy.start()
     kept_count = pos.shape[0]
     base[...] = jnp.zeros_like(base)
     base[pl.ds(0, 1), :] = jnp.full((1, LANES), SCAP * out_ref.shape[0], jnp.int32)
-    base[pl.ds(1, 1), pl.ds(0, ids.shape[1])] = ids[...]
+    for copy in copies:
+        copy.wait()
+    base[pl.ds(1, 1), pl.ds(0, a_ids.shape[1])] = a_ids[...]
+    base[pl.ds(2, 1), pl.ds(0, b_ids.shape[1])] = b_ids[...]
     out_ref[...] = jnp.broadcast_to(base[...][None], out_ref.shape)
     lane = lax.broadcasted_iota(jnp.int32, (1, LANES), 1)
 
@@ -41,29 +55,38 @@
     lax.fori_loop(0, out_ref.shape[0], clear, 0, unroll=8)
 
     def tell(q, carry):
-        owner = told[q]
+        owner = owners[q]
         order = sent[owner]
-        pos[q] = owner * SCAP + order
+        pos[q] = by_column(owner, row_count, col_count) * SCAP + order
         sent[owner] = order + 1
-        out_ref[owner, pl.ds(0, 1), :] = jnp.where(lane == order, told[kept_count + q], out_ref[owner, pl.ds(0, 1), :])
+        out_ref[owner, pl.ds(0, 1), :] = jnp.where(lane == order, slots[q], out_ref[owner, pl.ds(0, 1), :])
         return carry
 
     lax.fori_loop(0, kept_count, tell, 0)
 
 
-def announce(device_count, owners, slots, a_ids, b_ids):
-    return pl.pallas_call(
-        announce_kernel,
+def announce(row_count, col_count, owners, slots, a_ids, b_ids):
+    inputs = [pltpu.with_memory_space_constraint(array, pltpu.HBM) for array in (owners, slots, a_ids, b_ids)]
+    return pl.pallas_call(
+        functools.partial(announce_kernel, row_count, col_count),
         out_shape=[
-            pltpu.VMEM((device_count, EXCHANGE_ROWS, LANES), jnp.int32),
+            pltpu.VMEM((row_count * col_count, EXCHANGE_ROWS, LANES), jnp.int32),
             jax.ShapeDtypeStruct(owners.shape, jnp.int32),
         ],
-        in_specs=[SMEM, VMEM],
+        in_specs=[HBM] * 4,
         out_specs=[VMEM, SMEM],
-        scratch_shapes=[pltpu.VMEM((EXCHANGE_ROWS, LANES), jnp.int32), pltpu.SMEM((device_count,), jnp.int32)],
+        scratch_shapes=[
+            pltpu.VMEM((EXCHANGE_ROWS, LANES), jnp.int32),
+            pltpu.SMEM((row_count * col_count,), jnp.int32),
+            pltpu.SMEM(owners.shape, jnp.int32),
+            pltpu.SMEM(slots.shape, jnp.int32),
+            pltpu.VMEM(a_ids.shape, jnp.int32),
+            pltpu.VMEM(b_ids.shape, jnp.int32),
+            pltpu.SemaphoreType.DMA((4,)),
+        ],
         compiler_params=limit(2),
         name="announce",
-    )(jnp.concatenate([owners, slots]), jnp.concatenate([a_ids, b_ids], axis=1))
+    )(*inputs)
 
 
 def choose_kernel(cuts, where, *refs):
@@ -100,6 +123,29 @@
     )(where, *(piece for pair in pairs for piece in pair), after)
 
 
+def cut_kernel(piece, *refs):
+    out_refs, sems = refs[:-1], refs[-1]
+    size = out_refs[0].shape[0]
+    copies = [pltpu.make_async_copy(piece.at[pl.ds(n * size, size)], out, sems.at[n]) for n, out in enumerate(out_refs)]
+    for copy in copies:
+        copy.start()
+    for copy in copies:
+        copy.wait()
+
+
+def cut(piece):
+    part = pltpu.VMEM((piece.shape[0] // PARTS, piece.shape[1]), piece.dtype)
+    return pl.pallas_call(
+        cut_kernel,
+        out_shape=[part] * PARTS,
+        in_specs=[ANY],
+        out_specs=[VMEM] * PARTS,
+        scratch_shapes=[pltpu.SemaphoreType.DMA((PARTS,))],
+        compiler_params=limit(2),
+        name="cut",
+    )(piece)
+
+
 def tie_kernel(*refs):
     pass
 
@@ -220,8 +266,7 @@
         rows = exchange[member * col_count + j, pl.ds(1, 1), :]
         ids[pl.ds(half_panel, 1), :] = rows if half == 0 else pltpu.roll(rows, LANES - half * b_slots, 1)
         source = half * row_count + (member + j - i + row_count) % row_count
-        cols = exchange[i * col_count + source, pl.ds(1, 1), :]
-        ids[pl.ds(col_count + half_panel, 1), :] = pltpu.roll(cols, LANES - halves * b_slots, 1)
+        ids[pl.ds(col_count + half_panel, 1), :] = exchange[i * col_count + source, pl.ds(2, 1), :]
     rows = ids[pl.ds(0, col_count), :] * panel_width
     cols = ids[pl.ds(col_count, col_count), :]
     even = lax.broadcasted_iota(jnp.int32, cols.shape, 1) % 2 == 0
@@ -276,7 +321,7 @@
 
     def mark(d, carry):
         for m in range(SCAP):
-            plan[layout.source + slot_table[d, m]] = d * SCAP + m
+            plan[layout.source + slot_table[d, m]] = by_column(d, row_count, col_count) * SCAP + m
         return carry
 
     lax.fori_loop(0, row_count * col_count, mark, 0, unroll=8)
@@ -309,7 +354,7 @@
             pltpu.SemaphoreType.DMA((2,)),
         ],
         compiler_params=limit(26),
-        cost_estimate=pl.CostEstimate(flops=5 * 10**9, bytes_accessed=0, transcendentals=0),
+        cost_estimate=pl.CostEstimate(flops=1, bytes_accessed=0, transcendentals=0),
         name="first_products",
     )(keep, pos, where, exchange, *pieces)
 
@@ -414,11 +459,8 @@
     for _ in range(2, chips // 2):
         below.append(moved(below[-1], lambda d, c: around(d, c, 1)))
         above.append(moved(above[-1], lambda d, c: around(d, c, -1)))
-    pairs = [(below[-1], above[-1])] + [(piece, beside) for piece in ahead]
-    cuts = [PARTS] + [1] * len(ahead)
-    chosen = choose(where, pairs, cuts, exchange)
-    passed, crossing = chosen[:PARTS], chosen[PARTS:]
-    opposite = [moved(part, lambda d, c: around(d, c, 1 if c % CORES == 0 else -1)) for part in passed]
+    crossing = choose(where, [(piece, beside) for piece in ahead], [1] * len(ahead), exchange)
+    opposite = moved(above[-1], lambda d, c: around(d, c, -1))
     diagonal = [
         moved(piece, lambda d, c, shift=shift: (d ^ 1, c) if c % CORES == 0 else along(d, c, shift))
         for shift, piece in zip(shifts, crossing)
@@ -428,23 +470,25 @@
     for piece in (b_own, below[0], above[0]):
         near += [piece, swapped(piece)]
     *buffers, plan = multiply_near(exchange, near)
-    opposite[-1] = tied(opposite[-1], plan)
+    opposite = list(cut(tied(opposite, plan)))
+    crossed = [swapped(opposite[0])]
+    opposite[1] = tied(opposite[1], crossed[0])
+    crossed.append(swapped(opposite[1]))
     far = list(diagonal)
     for n in range(1, chips // 2 - 1):
         far += [below[n], swapped(below[n]), above[n], swapped(above[n])]
-    return buffers, plan, far + opposite + [swapped(part) for part in opposite]
+    return buffers, plan, far + opposite + crossed
 
 
 def body(a_blocks, a_rows, b_blocks, b_cols, c_keep, c_owner, c_slot):
     row_count = lax.axis_size("row")
     col_count = lax.axis_size("col")
-    device_count = row_count * col_count
     block = a_blocks.shape[-1]
     keep, owner_ids, slot_ids = c_keep[0, 0], c_owner[0, 0], c_slot[0, 0]
     sizes = (row_count, col_count, b_cols.shape[1])
     where = jnp.stack([lax.axis_index("row"), lax.axis_index("col")]).astype(jnp.int32)
 
-    outgoing, pos = announce(device_count, owner_ids, slot_ids, a_rows, b_cols)
+    outgoing, pos = announce(row_count, col_count, owner_ids, slot_ids, a_rows, b_cols)
 
     buffers, plan, far = gathered(
         a_blocks[0].reshape(-1, block),
@@ -456,7 +500,7 @@
         functools.partial(first_products, sizes, keep, pos, where),
     )
     send = rest_products(sizes, keep.shape[0], plan, buffers, far)
-    recv = lax.all_to_all(send, ("row", "col"), split_axis=0, concat_axis=0, tiled=True)
+    recv = lax.all_to_all(send, ("col", "row"), split_axis=0, concat_axis=0, tiled=True)
     return place(Layout(*sizes, keep.shape[0]), plan, recv)[None]
 
 

time: 110 us -> 108 us (0.982)
  waiting for transfers between devices: 26.7 us -> 24 us
  starting transfers between devices: 16.7 us -> 18.8 us
  other arithmetic: 1.57 us -> 0.07 us
    ppermute x12 -> x11, waiting for transfers between devices: 25.7 us -> 22.8 us  [moved(): lax.ppermute(piece, ('row', 'col'), [(d * col_count + c, to[0] * col_coun...]
    ppermute x12 -> x11, starting transfers between devices: 12.5 us -> 14.6 us  [moved(): lax.ppermute(piece, ('row', 'col'), [(d * col_count + c, to[0] * col_coun...]
    concatenate x2 -> x0, other arithmetic: 1.49 us -> none  [the longest x1 0.75 us: announce(): jnp.concatenate([a_ids, b_ids], axis=1)]
  transfers between devices with their start and end apart: 13 -> 12, of which waited for: 6 -> 7; matrix products, arithmetic and copies ran while one was open for 1% -> 0% of each run, Pallas kernels for 7% -> 7%
where the time goes in v2:
time: 108 us
  blocking collectives  53.3 us (49%)
  waiting for transfers between devices  24 us (22%)
  starting transfers between devices  18.8 us (17%)
  Pallas kernels  11.6 us (11%)
    all_to_all x1, blocking collectives, body(): lax.all_to_all(send, ('col', 'row'), split_axis=0, concat_axis=0, tiled=T...  53.3 us
    ppermute x11, waiting for transfers between devices, moved(): lax.ppermute(piece, ('row', 'col'), [(d * col_count + c, to[0] * col_coun...  22.8 us
    ppermute x11, starting transfers between devices, moved(): lax.ppermute(piece, ('row', 'col'), [(d * col_count + c, to[0] * col_coun...  14.6 us
    pallas_call x1, Pallas kernels, first_products(): pl.pallas_call(functools.partial(first_kernel, sizes, len(pieces)), out_s...  4.86 us
    all_to_all x1, starting transfers between devices, gathered(): lax.all_to_all(outgoing, ('row', 'col'), split_axis=0, concat_axis=0, til...  4.19 us
    pallas_call x1, Pallas kernels, rest_products(): pl.pallas_call(functools.partial(rest_kernel, sizes, len(pieces)), out_sh...  2.38 us
  transfers between devices with their start and end apart: 12, of which 7 were waited for; matrix products, arithmetic and copies ran while one was open for 0% of the time, Pallas kernels for 7%

profile of v2, /device:TPU:0, one launch (start us, length us, event | category | flops | bytes accessed | tf_op | source)
XLA Modules:
  0.0 107.8 jit_solution(5437502081452669815)
XLA Ops:
  0.0 3.0 %collective-permute-start.1 = (bf16[4096,128]{1,0:T(8,128)(2,1)}, bf16[4096,128]{1,0:T(8,128)(2,1)S(1)}, u32[]{:S(2)}, u32[]{:S(2)}) collective-permute-start(bf16[4096,128]{1,0:T(8,128)(2,1)} %bitcast.8), channel_id=1, source_target_pairs={{0,16},{1,17},{2,18},{3,19},{4,20},{5,21},{6,22},{7,23},{8,24},{9,... | collective-permute-start | bytes 3145736 | tf_op jit(solution)/shard_map/ppermute | solution.py:440
  3.0 1.5 %collective-permute-start = (bf16[4096,128]{1,0:T(8,128)(2,1)}, bf16[4096,128]{1,0:T(8,128)(2,1)S(1)}, u32[]{:S(2)}, u32[]{:S(2)}) collective-permute-start(bf16[4096,128]{1,0:T(8,128)(2,1)} %bitcast.9), channel_id=1, source_target_pairs={{0,8},{1,9},{2,10},{3,11},{4,12},{5,13},{6,14},{7,15},{8,0},{9,1},... | collective-permute-start | bytes 3145736 | tf_op jit(solution)/shard_map/ppermute | solution.py:440
  4.5 3.6 %collective-permute-start.5 = (bf16[2048,128]{1,0:T(8,128)(2,1)}, bf16[2048,128]{1,0:T(8,128)(2,1)}, u32[]{:S(2)}, u32[]{:S(2)}) collective-permute-start(bf16[2048,128]{1,0:T(8,128)(2,1)} %bitcast.11), channel_id=1, source_target_pairs={{0,6},{1,7},{2,0},{3,1},{4,2},{5,3},{6,4},{7,5},{8,14},{9,15},{10,... | collective-permute-start | bytes 1572872 | tf_op jit(solution)/shard_map/ppermute | solution.py:440
  8.1 1.8 %announce.1 = (s32[32,8,128]{2,1,0:T(8,128)}, s32[24]{0:T(128)S(1)}) custom-call(s32[24]{0:T(128)} %bitcast.16, s32[24]{0:T(128)} %bitcast.17, s32[1,32]{1,0:T(1,128)} %a_ids_ref.1, s32[1,16]{1,0:T(1,128)} %b_ids_ref.1), custom_call_target="tpu_custom_call" | custom-call | tf_op jit(solution)/shard_map/announce/pallas_call | solution.py:70
  9.8 4.2 %all-to-all-start = ((s32[32,8,128]{2,1,0:T(8,128)}), s32[32,8,128]{2,1,0:T(8,128)S(1)}, u32[]{:S(2)}, u32[]{:S(2)}) async-start(s32[32,8,128]{2,1,0:T(8,128)} %get-tuple-element.15), calls=%async_computation | async-start | bytes 262144 | tf_op jit(solution)/shard_map/all_to_all | solution.py:458
  14.0 0.3 collective-permute-start.2
  14.4 6.4 %collective-permute-done.5.refs_7_ = bf16[2048,128]{1,0:T(8,128)(2,1)} collective-permute-done((bf16[2048,128]{1,0:T(8,128)(2,1)}, bf16[2048,128]{1,0:T(8,128)(2,1)}, u32[]{:S(2)}, u32[]{:S(2)}) %collective-permute-start.5) | collective-permute-done | bytes 524320 | tf_op jit(solution)/shard_map/ppermute | solution.py:440
  20.8 4.3 %collective-permute-start.8 = (bf16[2048,128]{1,0:T(8,128)(2,1)}, bf16[2048,128]{1,0:T(8,128)(2,1)S(1)}, u32[]{:S(2)}, u32[]{:S(2)}) collective-permute-start(bf16[2048,128]{1,0:T(8,128)(2,1)} %collective-permute-done.5.refs_7_), channel_id=1, source_target_pairs={{0,6},{1,7},{2,0},{3,1},{4,2},{5,3},{6,4},{7,5},{8,14},{9,15},{10,... | collective-permute-start | bytes 1572872 | tf_op jit(solution)/shard_map/ppermute | solution.py:440
  25.0 7.9 %collective-permute-done.3.refs_5_ = bf16[2048,128]{1,0:T(8,128)(2,1)} collective-permute-done((bf16[2048,128]{1,0:T(8,128)(2,1)}, bf16[2048,128]{1,0:T(8,128)(2,1)}, u32[]{:S(2)}, u32[]{:S(2)}) %collective-permute-start.3) | collective-permute-done | bytes 524320 | tf_op jit(solution)/shard_map/ppermute | solution.py:440
  33.0 0.5 collective-permute-start.4
  33.5 0.1 pad_add_fusion.where
  33.5 1.2 %all-to-all-done.exchange.refs_2_ = s32[32,8,128]{2,1,0:T(8,128)S(1)} async-done(((s32[32,8,128]{2,1,0:T(8,128)}), s32[32,8,128]{2,1,0:T(8,128)S(1)}, u32[]{:S(2)}, u32[]{:S(2)}) %all-to-all-start) | async-done | bytes 131104 | tf_op jit(solution)/shard_map/all_to_all | solution.py:458
  34.8 0.6 choose.1
  35.4 1.2 %collective-permute-start.7 = (bf16[4096,128]{1,0:T(8,128)(2,1)S(1)}, bf16[4096,128]{1,0:T(8,128)(2,1)S(1)}, u32[]{:S(2)}, u32[]{:S(2)}) collective-permute-start(bf16[4096,128]{1,0:T(8,128)(2,1)S(1)} %choose.1), channel_id=1, source_target_pairs={{0,8},{1,17},{2,10},{3,19},{4,12},{5,21},{6,14},{7,23},{8,0},{9,25... | collective-permute-start | bytes 3145736 | tf_op jit(solution)/shard_map/ppermute | solution.py:440
  36.7 4.9 %first_products.1 = (bf16[16384,128]{1,0:T(8,128)(2,1)S(1)}, bf16[16384,128]{1,0:T(8,128)(2,1)S(1)}, f32[25,128,128]{2,1,0:T(8,128)S(1)}, s32[356]{0:T(512)S(1)}) custom-call(s32[24]{0:T(128)S(1)} %bitcast.15, s32[24]{0:T(128)S(1)} %get-tuple-element.14.pos, s32[2]{0:T(128)S(1)} %pad_add_fusion.where, s32[32,8,128]{2,1,0:T(8,128)S(1)} %all-to-all-done.exchange.refs_2_, ...), custom_call_target="tpu_custom_call" | custom-call | flops 1 | tf_op jit(solution)/shard_map/first_products/pallas_call | solution.py:336
  41.5 2.1 %collective-permute-done.8.refs_0_ = bf16[2048,128]{1,0:T(8,128)(2,1)S(1)} collective-permute-done((bf16[2048,128]{1,0:T(8,128)(2,1)}, bf16[2048,128]{1,0:T(8,128)(2,1)S(1)}, u32[]{:S(2)}, u32[]{:S(2)}) %collective-permute-start.8) | collective-permute-done | bytes 524320 | tf_op jit(solution)/shard_map/ppermute | solution.py:440
  43.7 0.1 collective-permute-start.9
  43.8 1.5 %collective-permute-done.9.refs_1_.refs_6_ = bf16[1024,128]{1,0:T(8,128)(2,1)S(1)} collective-permute-done((bf16[1024,128]{1,0:T(8,128)(2,1)S(1)}, bf16[1024,128]{1,0:T(8,128)(2,1)S(1)}, u32[]{:S(2)}, u32[]{:S(2)}) %collective-permute-start.9) | collective-permute-done | bytes 262176 | tf_op jit(solution)/shard_map/ppermute | solution.py:440
  45.3 0.1 collective-permute-start.10
  45.4 1.4 %collective-permute-done.10.refs_7_ = bf16[1024,128]{1,0:T(8,128)(2,1)S(1)} collective-permute-done((bf16[1024,128]{1,0:T(8,128)(2,1)S(1)}, bf16[1024,128]{1,0:T(8,128)(2,1)S(1)}, u32[]{:S(2)}, u32[]{:S(2)}) %collective-permute-start.10) | collective-permute-done | bytes 262176 | tf_op jit(solution)/shard_map/ppermute | solution.py:440
  46.8 3.5 %collective-permute-done.7.refs_3_ = bf16[4096,128]{1,0:T(8,128)(2,1)S(1)} collective-permute-done((bf16[4096,128]{1,0:T(8,128)(2,1)S(1)}, bf16[4096,128]{1,0:T(8,128)(2,1)S(1)}, u32[]{:S(2)}, u32[]{:S(2)}) %collective-permute-start.7) | collective-permute-done | bytes 1048608 | tf_op jit(solution)/shard_map/ppermute | solution.py:440
  50.3 2.4 %rest_products.1 = (bf16[16384,128]{1,0:T(8,128)(2,1)S(1)}, bf16[16384,128]{1,0:T(8,128)(2,1)S(1)}, f32[25,128,128]{2,1,0:T(8,128)S(1)}, bf16[64,128,128]{2,1,0:T(8,128)(2,1)}) custom-call(s32[356]{0:T(512)S(1)} %get-tuple-element.16.refs_1_.plan, ...), custom_call_target="tpu_custom_call", output_to_operand_aliasing={{0}: (1, {}), {1}: (2, {}), {2}: (3, {})} | custom-call | tf_op jit(solution)/shard_map/rest_products/pallas_call | solution.py:385
  52.7 53.3 %all_to_all.10.recv_ref = bf16[64,128,128]{2,1,0:T(8,128)(2,1)S(1)} all-to-all(bf16[64,128,128]{2,1,0:T(8,128)(2,1)} %get-tuple-element.22), channel_id=1, replica_groups=mesh['row'=4,'col'=8] {'col','row'}, dimensions={0} | all-to-all | bytes 4194304 | tf_op jit(solution)/shard_map/all_to_all | solution.py:503
  106.0 1.9 %place.1 = bf16[64,128,128]{2,1,0:T(8,128)(2,1)} custom-call(s32[356]{0:T(512)S(1)} %get-tuple-element.16.refs_1_.plan, bf16[64,128,128]{2,1,0:T(8,128)(2,1)S(1)} %all_to_all.10.recv_ref), custom_call_target="tpu_custom_call" | custom-call | tf_op jit(solution)/shard_map/place/pallas_call | solution.py:424
  (16 shorter events, 0.1 us)
Async XLA Ops:
  0.0 36.6 %copy-start.1 = (bf16[1,16,128,128]{3,2,1,0:T(8,128)(2,1)S(1)}, bf16[1,16,128,128]{3,2,1,0:T(8,128)(2,1)}, u32[]{:S(2)}) copy-start(bf16[1,16,128,128]{3,2,1,0:T(8,128)(2,1)} %param.9) | copy-start | bytes 1572868
  0.0 36.7 %copy-start.2 = (s32[1,1,24]{2,1,0:T(1,128)S(1)}, s32[1,1,24]{2,1,0:T(1,128)}, u32[]{:S(2)}) copy-start(s32[1,1,24]{2,1,0:T(1,128)} %param.11) | copy-start | bytes 292
  0.0 33.0 %collective-permute-start.1 = (bf16[4096,128]{1,0:T(8,128)(2,1)}, bf16[4096,128]{1,0:T(8,128)(2,1)S(1)}, u32[]{:S(2)}, u32[]{:S(2)}) collective-permute-start(bf16[4096,128]{1,0:T(8,128)(2,1)} %bitcast.8), channel_id=1, source_target_pairs={{0,16},{1,17},{2,18},{3,19},{4,20},{5,21},{6,22},{7,23},{8,24},{9,... | collective-permute-start | bytes 3145736 | tf_op jit(solution)/shard_map/ppermute | solution.py:440
  3.0 31.8 %collective-permute-start = (bf16[4096,128]{1,0:T(8,128)(2,1)}, bf16[4096,128]{1,0:T(8,128)(2,1)S(1)}, u32[]{:S(2)}, u32[]{:S(2)}) collective-permute-start(bf16[4096,128]{1,0:T(8,128)(2,1)} %bitcast.9), channel_id=1, source_target_pairs={{0,8},{1,9},{2,10},{3,11},{4,12},{5,13},{6,14},{7,15},{8,0},{9,1},... | collective-permute-start | bytes 3145736 | tf_op jit(solution)/shard_map/ppermute | solution.py:440
  4.5 16.3 %collective-permute-start.5 = (bf16[2048,128]{1,0:T(8,128)(2,1)}, bf16[2048,128]{1,0:T(8,128)(2,1)}, u32[]{:S(2)}, u32[]{:S(2)}) collective-permute-start(bf16[2048,128]{1,0:T(8,128)(2,1)} %bitcast.11), channel_id=1, source_target_pairs={{0,6},{1,7},{2,0},{3,1},{4,2},{5,3},{6,4},{7,5},{8,14},{9,15},{10,... | collective-permute-start | bytes 1572872 | tf_op jit(solution)/shard_map/ppermute | solution.py:440
  8.1 24.9 %collective-permute-start.3 = (bf16[2048,128]{1,0:T(8,128)(2,1)}, bf16[2048,128]{1,0:T(8,128)(2,1)}, u32[]{:S(2)}, u32[]{:S(2)}) collective-permute-start(bf16[2048,128]{1,0:T(8,128)(2,1)} %bitcast.12), channel_id=1, source_target_pairs={{0,2},{1,3},{2,4},{3,5},{4,6},{5,7},{6,0},{7,1},{8,10},{9,11},{10,... | collective-permute-start | bytes 1572872 | tf_op jit(solution)/shard_map/ppermute | solution.py:440
  9.8 24.9 %all-to-all-start = ((s32[32,8,128]{2,1,0:T(8,128)}), s32[32,8,128]{2,1,0:T(8,128)S(1)}, u32[]{:S(2)}, u32[]{:S(2)}) async-start(s32[32,8,128]{2,1,0:T(8,128)} %get-tuple-element.15), calls=%async_computation | async-start | bytes 262144 | tf_op jit(solution)/shard_map/all_to_all | solution.py:458
  14.0 22.6 %collective-permute-start.2 = (bf16[2048,128]{1,0:T(8,128)(2,1)}, bf16[2048,128]{1,0:T(8,128)(2,1)}, u32[]{:S(2)}, u32[]{:S(2)}) collective-permute-start(bf16[2048,128]{1,0:T(8,128)(2,1)} %bitcast.13), channel_id=1, source_target_pairs={{0,1},{1,0},{2,3},{3,2},{4,5},{5,4},{6,7},{7,6},{8,9},{9,8},{10,11... | collective-permute-start | bytes 1572872 | tf_op jit(solution)/shard_map/ppermute | solution.py:440
  20.8 22.9 %collective-permute-start.8 = (bf16[2048,128]{1,0:T(8,128)(2,1)}, bf16[2048,128]{1,0:T(8,128)(2,1)S(1)}, u32[]{:S(2)}, u32[]{:S(2)}) collective-permute-start(bf16[2048,128]{1,0:T(8,128)(2,1)} %collective-permute-done.5.refs_7_), channel_id=1, source_target_pairs={{0,6},{1,7},{2,0},{3,1},{4,2},{5,3},{6,4},{7,5},{8,14},{9,15},{10,... | collective-permute-start | bytes 1572872 | tf_op jit(solution)/shard_map/ppermute | solution.py:440
  33.0 3.7 %collective-permute-start.6 = (bf16[2048,128]{1,0:T(8,128)(2,1)}, bf16[2048,128]{1,0:T(8,128)(2,1)}, u32[]{:S(2)}, u32[]{:S(2)}) collective-permute-start(bf16[2048,128]{1,0:T(8,128)(2,1)} %collective-permute-done.5.refs_7_), channel_id=1, source_target_pairs={{0,1},{1,0},{2,3},{3,2},{4,5},{5,4},{6,7},{7,6},{8,9},{9,8},{10,11... | collective-permute-start | bytes 1572872 | tf_op jit(solution)/shard_map/ppermute | solution.py:440
  33.0 3.7 %collective-permute-start.4 = (bf16[2048,128]{1,0:T(8,128)(2,1)}, bf16[2048,128]{1,0:T(8,128)(2,1)}, u32[]{:S(2)}, u32[]{:S(2)}) collective-permute-start(bf16[2048,128]{1,0:T(8,128)(2,1)} %collective-permute-done.3.refs_5_), channel_id=1, source_target_pairs={{0,1},{1,0},{2,3},{3,2},{4,5},{5,4},{6,7},{7,6},{8,9},{9,8},{10,11... | collective-permute-start | bytes 1572872 | tf_op jit(solution)/shard_map/ppermute | solution.py:440
  34.8 1.9 %copy-start = (bf16[1,32,128,128]{3,2,1,0:T(8,128)(2,1)S(1)}, bf16[1,32,128,128]{3,2,1,0:T(8,128)(2,1)}, u32[]{:S(2)}) copy-start(bf16[1,32,128,128]{3,2,1,0:T(8,128)(2,1)} %param.7) | copy-start | bytes 3145732
  35.4 14.9 %collective-permute-start.7 = (bf16[4096,128]{1,0:T(8,128)(2,1)S(1)}, bf16[4096,128]{1,0:T(8,128)(2,1)S(1)}, u32[]{:S(2)}, u32[]{:S(2)}) collective-permute-start(bf16[4096,128]{1,0:T(8,128)(2,1)S(1)} %choose.1), channel_id=1, source_target_pairs={{0,8},{1,17},{2,10},{3,19},{4,12},{5,21},{6,14},{7,23},{8,0},{9,25... | collective-permute-start | bytes 3145736 | tf_op jit(solution)/shard_map/ppermute | solution.py:440
  43.7 1.6 %collective-permute-start.9 = (bf16[1024,128]{1,0:T(8,128)(2,1)S(1)}, bf16[1024,128]{1,0:T(8,128)(2,1)S(1)}, u32[]{:S(2)}, u32[]{:S(2)}) collective-permute-start(bf16[1024,128]{1,0:T(8,128)(2,1)S(1)} %get-tuple-element.20.refs_4_), channel_id=1, source_target_pairs={{0,1},{1,0},{2,3},{3,2},{4,5},{5,4},{6,7},{7,6},{8,9},{9,8},{10,11... | collective-permute-start | bytes 786440 | tf_op jit(solution)/shard_map/ppermute | solution.py:440
  45.3 1.5 %collective-permute-start.10 = (bf16[1024,128]{1,0:T(8,128)(2,1)S(1)}, bf16[1024,128]{1,0:T(8,128)(2,1)S(1)}, u32[]{:S(2)}, u32[]{:S(2)}) collective-permute-start(bf16[1024,128]{1,0:T(8,128)(2,1)S(1)} %tied.3.refs_5_), channel_id=1, source_target_pairs={{0,1},{1,0},{2,3},{3,2},{4,5},{5,4},{6,7},{7,6},{8,9},{9,8},{10,11... | collective-permute-start | bytes 786440 | tf_op jit(solution)/shard_map/ppermute | solution.py:440

commit v3 on v2

--- a/solution.py
+++ b/solution.py
@@ -30,21 +30,11 @@
     return device % col_count * row_count + device // col_count
 
 
-def announce_kernel(
-    row_count, col_count, owners_ref, slots_ref, a_ids_ref, b_ids_ref, out_ref, pos,
-    base, sent, owners, slots, a_ids, b_ids, sems,
-):
-    moves = [(owners_ref, owners), (slots_ref, slots), (a_ids_ref, a_ids), (b_ids_ref, b_ids)]
-    copies = [pltpu.make_async_copy(source, target, sems.at[n]) for n, (source, target) in enumerate(moves)]
-    for copy in copies:
-        copy.start()
+def announce_kernel(row_count, col_count, told, ids, out_ref, pos, base, sent):
     kept_count = pos.shape[0]
     base[...] = jnp.zeros_like(base)
     base[pl.ds(0, 1), :] = jnp.full((1, LANES), SCAP * out_ref.shape[0], jnp.int32)
-    for copy in copies:
-        copy.wait()
-    base[pl.ds(1, 1), pl.ds(0, a_ids.shape[1])] = a_ids[...]
-    base[pl.ds(2, 1), pl.ds(0, b_ids.shape[1])] = b_ids[...]
+    base[pl.ds(1, 1), pl.ds(0, ids.shape[1])] = ids[...]
     out_ref[...] = jnp.broadcast_to(base[...][None], out_ref.shape)
     lane = lax.broadcasted_iota(jnp.int32, (1, LANES), 1)
 
@@ -55,38 +45,30 @@
     lax.fori_loop(0, out_ref.shape[0], clear, 0, unroll=8)
 
     def tell(q, carry):
-        owner = owners[q]
+        owner = told[q]
         order = sent[owner]
         pos[q] = by_column(owner, row_count, col_count) * SCAP + order
         sent[owner] = order + 1
-        out_ref[owner, pl.ds(0, 1), :] = jnp.where(lane == order, slots[q], out_ref[owner, pl.ds(0, 1), :])
+        place = by_column(owner, row_count, col_count)
+        out_ref[place, pl.ds(0, 1), :] = jnp.where(lane == order, told[kept_count + q], out_ref[place, pl.ds(0, 1), :])
         return carry
 
     lax.fori_loop(0, kept_count, tell, 0)
 
 
 def announce(row_count, col_count, owners, slots, a_ids, b_ids):
-    inputs = [pltpu.with_memory_space_constraint(array, pltpu.HBM) for array in (owners, slots, a_ids, b_ids)]
     return pl.pallas_call(
         functools.partial(announce_kernel, row_count, col_count),
         out_shape=[
             pltpu.VMEM((row_count * col_count, EXCHANGE_ROWS, LANES), jnp.int32),
             jax.ShapeDtypeStruct(owners.shape, jnp.int32),
         ],
-        in_specs=[HBM] * 4,
+        in_specs=[SMEM, VMEM],
         out_specs=[VMEM, SMEM],
-        scratch_shapes=[
-            pltpu.VMEM((EXCHANGE_ROWS, LANES), jnp.int32),
-            pltpu.SMEM((row_count * col_count,), jnp.int32),
-            pltpu.SMEM(owners.shape, jnp.int32),
-            pltpu.SMEM(slots.shape, jnp.int32),
-            pltpu.VMEM(a_ids.shape, jnp.int32),
-            pltpu.VMEM(b_ids.shape, jnp.int32),
-            pltpu.SemaphoreType.DMA((4,)),
-        ],
+        scratch_shapes=[pltpu.VMEM((EXCHANGE_ROWS, LANES), jnp.int32), pltpu.SMEM((row_count * col_count,), jnp.int32)],
         compiler_params=limit(2),
         name="announce",
-    )(*inputs)
+    )(jnp.concatenate([owners, slots]), jnp.concatenate([a_ids, b_ids], axis=1))
 
 
 def choose_kernel(cuts, where, *refs):
@@ -263,10 +245,11 @@
     halves = col_count // row_count
     for half_panel in range(col_count):
         member, half = half_panel // halves, half_panel % halves
-        rows = exchange[member * col_count + j, pl.ds(1, 1), :]
+        rows = exchange[j * row_count + member, pl.ds(1, 1), :]
         ids[pl.ds(half_panel, 1), :] = rows if half == 0 else pltpu.roll(rows, LANES - half * b_slots, 1)
         source = half * row_count + (member + j - i + row_count) % row_count
-        ids[pl.ds(col_count + half_panel, 1), :] = exchange[i * col_count + source, pl.ds(2, 1), :]
+        cols = exchange[source * row_count + i, pl.ds(1, 1), :]
+        ids[pl.ds(col_count + half_panel, 1), :] = pltpu.roll(cols, LANES - halves * b_slots, 1)
     rows = ids[pl.ds(0, col_count), :] * panel_width
     cols = ids[pl.ds(col_count, col_count), :]
     even = lax.broadcasted_iota(jnp.int32, cols.shape, 1) % 2 == 0
@@ -321,7 +304,7 @@
 
     def mark(d, carry):
         for m in range(SCAP):
-            plan[layout.source + slot_table[d, m]] = by_column(d, row_count, col_count) * SCAP + m
+            plan[layout.source + slot_table[d, m]] = d * SCAP + m
         return carry
 
     lax.fori_loop(0, row_count * col_count, mark, 0, unroll=8)
@@ -455,7 +438,7 @@
     above = [moved(b_own, lambda d, c: around(d, c, -1))]
     beside = moved(a_own, lambda d, c: (d ^ 1, c))
     ahead = [moved(a_own, lambda d, c, shift=shift: along(d, c, shift)) for shift in shifts]
-    exchange = lax.all_to_all(outgoing, ("row", "col"), split_axis=0, concat_axis=0, tiled=True)
+    exchange = lax.all_to_all(outgoing, ("col", "row"), split_axis=0, concat_axis=0, tiled=True)
     for _ in range(2, chips // 2):
         below.append(moved(below[-1], lambda d, c: around(d, c, 1)))
         above.append(moved(above[-1], lambda d, c: around(d, c, -1)))

time: 108 us -> 108 us (level)
  other arithmetic: 0.07 us -> 1.57 us
    concatenate x0 -> x2, other arithmetic: none -> 1.49 us  [the longest x1 0.75 us: announce(): jnp.concatenate([a_ids, b_ids], axis=1)]
  transfers between devices with their start and end apart: 12 -> 12, of which waited for: 7 -> 7; matrix products, arithmetic and copies ran while one was open for 0% -> 1% of each run, Pallas kernels for 7% -> 7%
where the time goes in v3:
time: 108 us
  blocking collectives  53.7 us (50%)
  waiting for transfers between devices  23.1 us (21%)
  starting transfers between devices  18.3 us (17%)
  Pallas kernels  11.5 us (11%)
  other arithmetic  1.57 us (1%)
    all_to_all x1, blocking collectives, body(): lax.all_to_all(send, ('col', 'row'), split_axis=0, concat_axis=0, tiled=T...  53.7 us
    ppermute x11, waiting for transfers between devices, moved(): lax.ppermute(piece, ('row', 'col'), [(d * col_count + c, to[0] * col_coun...  21.9 us
    ppermute x11, starting transfers between devices, moved(): lax.ppermute(piece, ('row', 'col'), [(d * col_count + c, to[0] * col_coun...  14.1 us
    pallas_call x1, Pallas kernels, first_products(): pl.pallas_call(functools.partial(first_kernel, sizes, len(pieces)), out_s...  5 us
    all_to_all x1, starting transfers between devices, gathered(): lax.all_to_all(outgoing, ('col', 'row'), split_axis=0, concat_axis=0, til...  4.19 us
    pallas_call x1, Pallas kernels, rest_products(): pl.pallas_call(functools.partial(rest_kernel, sizes, len(pieces)), out_sh...  2.38 us
  transfers between devices with their start and end apart: 12, of which 7 were waited for; matrix products, arithmetic and copies ran while one was open for 1% of the time, Pallas kernels for 7%

profile of v3, /device:TPU:0, one launch (start us, length us, event | category | flops | bytes accessed | tf_op | source)
XLA Modules:
  0.0 108.2 jit_solution(10536748791234512307)
XLA Ops:
  0.0 3.0 %collective-permute-start.1 = (bf16[4096,128]{1,0:T(8,128)(2,1)}, bf16[4096,128]{1,0:T(8,128)(2,1)S(1)}, u32[]{:S(2)}, u32[]{:S(2)}) collective-permute-start(bf16[4096,128]{1,0:T(8,128)(2,1)} %bitcast.8), channel_id=1, source_target_pairs={{0,16},{1,17},{2,18},{3,19},{4,20},{5,21},{6,22},{7,23},{8,24},{9,... | collective-permute-start | bytes 3145736 | tf_op jit(solution)/shard_map/ppermute | solution.py:423
  3.0 1.5 %collective-permute-start = (bf16[4096,128]{1,0:T(8,128)(2,1)}, bf16[4096,128]{1,0:T(8,128)(2,1)S(1)}, u32[]{:S(2)}, u32[]{:S(2)}) collective-permute-start(bf16[4096,128]{1,0:T(8,128)(2,1)} %bitcast.9), channel_id=1, source_target_pairs={{0,8},{1,9},{2,10},{3,11},{4,12},{5,13},{6,14},{7,15},{8,0},{9,1},... | collective-permute-start | bytes 3145736 | tf_op jit(solution)/shard_map/ppermute | solution.py:423
  4.5 3.6 %collective-permute-start.5 = (bf16[2048,128]{1,0:T(8,128)(2,1)}, bf16[2048,128]{1,0:T(8,128)(2,1)}, u32[]{:S(2)}, u32[]{:S(2)}) collective-permute-start(bf16[2048,128]{1,0:T(8,128)(2,1)} %bitcast.11), channel_id=1, source_target_pairs={{0,6},{1,7},{2,0},{3,1},{4,2},{5,3},{6,4},{7,5},{8,14},{9,15},{10,... | collective-permute-start | bytes 1572872 | tf_op jit(solution)/shard_map/ppermute | solution.py:423
  8.1 0.7 pad_add_fusion.1.ids
  8.8 0.7 pad_add_fusion.told
  9.6 1.6 %announce.1 = (s32[32,8,128]{2,1,0:T(8,128)}, s32[24]{0:T(128)S(1)}) custom-call(s32[48]{0:T(128)S(1)} %pad_add_fusion.told, s32[1,48]{1,0:T(1,128)S(1)} %pad_add_fusion.1.ids), custom_call_target="tpu_custom_call" | custom-call | tf_op jit(solution)/shard_map/announce/pallas_call | solution.py:60
  11.1 4.2 %all-to-all-start = ((s32[32,8,128]{2,1,0:T(8,128)}), s32[32,8,128]{2,1,0:T(8,128)S(1)}, u32[]{:S(2)}, u32[]{:S(2)}) async-start(s32[32,8,128]{2,1,0:T(8,128)} %get-tuple-element.15), calls=%async_computation | async-start | bytes 262144 | tf_op jit(solution)/shard_map/all_to_all | solution.py:441
  15.3 0.3 collective-permute-start.2
  15.7 5.1 %collective-permute-done.5.refs_7_ = bf16[2048,128]{1,0:T(8,128)(2,1)} collective-permute-done((bf16[2048,128]{1,0:T(8,128)(2,1)}, bf16[2048,128]{1,0:T(8,128)(2,1)}, u32[]{:S(2)}, u32[]{:S(2)}) %collective-permute-start.5) | collective-permute-done | bytes 524320 | tf_op jit(solution)/shard_map/ppermute | solution.py:423
  20.8 4.3 %collective-permute-start.8 = (bf16[2048,128]{1,0:T(8,128)(2,1)}, bf16[2048,128]{1,0:T(8,128)(2,1)S(1)}, u32[]{:S(2)}, u32[]{:S(2)}) collective-permute-start(bf16[2048,128]{1,0:T(8,128)(2,1)} %collective-permute-done.5.refs_7_), channel_id=1, source_target_pairs={{0,6},{1,7},{2,0},{3,1},{4,2},{5,3},{6,4},{7,5},{8,14},{9,15},{10,... | collective-permute-start | bytes 1572872 | tf_op jit(solution)/shard_map/ppermute | solution.py:423
  25.0 7.9 %collective-permute-done.3.refs_5_ = bf16[2048,128]{1,0:T(8,128)(2,1)} collective-permute-done((bf16[2048,128]{1,0:T(8,128)(2,1)}, bf16[2048,128]{1,0:T(8,128)(2,1)}, u32[]{:S(2)}, u32[]{:S(2)}) %collective-permute-start.3) | collective-permute-done | bytes 524320 | tf_op jit(solution)/shard_map/ppermute | solution.py:423
  33.0 0.5 collective-permute-start.4
  33.5 1.2 %all-to-all-done.exchange.refs_2_ = s32[32,8,128]{2,1,0:T(8,128)S(1)} async-done(((s32[32,8,128]{2,1,0:T(8,128)}), s32[32,8,128]{2,1,0:T(8,128)S(1)}, u32[]{:S(2)}, u32[]{:S(2)}) %all-to-all-start) | async-done | bytes 131104 | tf_op jit(solution)/shard_map/all_to_all | solution.py:441
  34.8 0.6 choose.1
  35.4 0.7 collective-permute-start.7
  36.2 5.0 %first_products.1 = (bf16[16384,128]{1,0:T(8,128)(2,1)S(1)}, bf16[16384,128]{1,0:T(8,128)(2,1)S(1)}, f32[25,128,128]{2,1,0:T(8,128)S(1)}, s32[356]{0:T(512)S(1)}) custom-call(s32[24]{0:T(128)S(1)} %bitcast.15, s32[24]{0:T(128)S(1)} %get-tuple-element.14.pos, s32[2]{0:T(128)S(1)} %pad_add_fusion.2.where, s32[32,8,128]{2,1,0:T(8,128)S(1)} %all-to-all-done.exchange.refs_2_, ...), custom_call_target="tpu_custom_call" | custom-call | flops 1 | tf_op jit(solution)/shard_map/first_products/pallas_call | solution.py:319
  41.2 2.5 %collective-permute-done.8.refs_0_ = bf16[2048,128]{1,0:T(8,128)(2,1)S(1)} collective-permute-done((bf16[2048,128]{1,0:T(8,128)(2,1)}, bf16[2048,128]{1,0:T(8,128)(2,1)S(1)}, u32[]{:S(2)}, u32[]{:S(2)}) %collective-permute-start.8) | collective-permute-done | bytes 524320 | tf_op jit(solution)/shard_map/ppermute | solution.py:423
  43.8 1.5 %collective-permute-done.9.refs_1_.refs_6_ = bf16[1024,128]{1,0:T(8,128)(2,1)S(1)} collective-permute-done((bf16[1024,128]{1,0:T(8,128)(2,1)S(1)}, bf16[1024,128]{1,0:T(8,128)(2,1)S(1)}, u32[]{:S(2)}, u32[]{:S(2)}) %collective-permute-start.9) | collective-permute-done | bytes 262176 | tf_op jit(solution)/shard_map/ppermute | solution.py:423
  45.3 0.1 collective-permute-start.10
  45.4 1.4 %collective-permute-done.10.refs_7_ = bf16[1024,128]{1,0:T(8,128)(2,1)S(1)} collective-permute-done((bf16[1024,128]{1,0:T(8,128)(2,1)S(1)}, bf16[1024,128]{1,0:T(8,128)(2,1)S(1)}, u32[]{:S(2)}, u32[]{:S(2)}) %collective-permute-start.10) | collective-permute-done | bytes 262176 | tf_op jit(solution)/shard_map/ppermute | solution.py:423
  46.8 3.5 %collective-permute-done.7.refs_3_ = bf16[4096,128]{1,0:T(8,128)(2,1)S(1)} collective-permute-done((bf16[4096,128]{1,0:T(8,128)(2,1)S(1)}, bf16[4096,128]{1,0:T(8,128)(2,1)S(1)}, u32[]{:S(2)}, u32[]{:S(2)}) %collective-permute-start.7) | collective-permute-done | bytes 1048608 | tf_op jit(solution)/shard_map/ppermute | solution.py:423
  50.3 2.4 %rest_products.1 = (bf16[16384,128]{1,0:T(8,128)(2,1)S(1)}, bf16[16384,128]{1,0:T(8,128)(2,1)S(1)}, f32[25,128,128]{2,1,0:T(8,128)S(1)}, bf16[64,128,128]{2,1,0:T(8,128)(2,1)}) custom-call(s32[356]{0:T(512)S(1)} %get-tuple-element.16.refs_1_.plan, ...), custom_call_target="tpu_custom_call", output_to_operand_aliasing={{0}: (1, {}), {1}: (2, {}), {2}: (3, {})} | custom-call | tf_op jit(solution)/shard_map/rest_products/pallas_call | solution.py:368
  52.7 53.7 %all_to_all.10.recv_ref = bf16[64,128,128]{2,1,0:T(8,128)(2,1)S(1)} all-to-all(bf16[64,128,128]{2,1,0:T(8,128)(2,1)} %get-tuple-element.22), channel_id=1, replica_groups=mesh['row'=4,'col'=8] {'col','row'}, dimensions={0} | all-to-all | bytes 4194304 | tf_op jit(solution)/shard_map/all_to_all | solution.py:486
  106.4 1.9 %place.1 = bf16[64,128,128]{2,1,0:T(8,128)(2,1)} custom-call(s32[356]{0:T(512)S(1)} %get-tuple-element.16.refs_1_.plan, bf16[64,128,128]{2,1,0:T(8,128)(2,1)S(1)} %all_to_all.10.recv_ref), custom_call_target="tpu_custom_call" | custom-call | tf_op jit(solution)/shard_map/place/pallas_call | solution.py:407
  (18 shorter events, 0.2 us)
Async XLA Ops:
  0.0 36.1 %copy-start.1 = (bf16[1,16,128,128]{3,2,1,0:T(8,128)(2,1)S(1)}, bf16[1,16,128,128]{3,2,1,0:T(8,128)(2,1)}, u32[]{:S(2)}) copy-start(bf16[1,16,128,128]{3,2,1,0:T(8,128)(2,1)} %param.9) | copy-start | bytes 1572868
  0.0 36.1 %copy-start.2 = (s32[1,1,24]{2,1,0:T(1,128)S(1)}, s32[1,1,24]{2,1,0:T(1,128)}, u32[]{:S(2)}) copy-start(s32[1,1,24]{2,1,0:T(1,128)} %param.11) | copy-start | bytes 292
  0.0 33.0 %collective-permute-start.1 = (bf16[4096,128]{1,0:T(8,128)(2,1)}, bf16[4096,128]{1,0:T(8,128)(2,1)S(1)}, u32[]{:S(2)}, u32[]{:S(2)}) collective-permute-start(bf16[4096,128]{1,0:T(8,128)(2,1)} %bitcast.8), channel_id=1, source_target_pairs={{0,16},{1,17},{2,18},{3,19},{4,20},{5,21},{6,22},{7,23},{8,24},{9,... | collective-permute-start | bytes 3145736 | tf_op jit(solution)/shard_map/ppermute | solution.py:423
  3.0 31.8 %collective-permute-start = (bf16[4096,128]{1,0:T(8,128)(2,1)}, bf16[4096,128]{1,0:T(8,128)(2,1)S(1)}, u32[]{:S(2)}, u32[]{:S(2)}) collective-permute-start(bf16[4096,128]{1,0:T(8,128)(2,1)} %bitcast.9), channel_id=1, source_target_pairs={{0,8},{1,9},{2,10},{3,11},{4,12},{5,13},{6,14},{7,15},{8,0},{9,1},... | collective-permute-start | bytes 3145736 | tf_op jit(solution)/shard_map/ppermute | solution.py:423
  4.5 16.3 %collective-permute-start.5 = (bf16[2048,128]{1,0:T(8,128)(2,1)}, bf16[2048,128]{1,0:T(8,128)(2,1)}, u32[]{:S(2)}, u32[]{:S(2)}) collective-permute-start(bf16[2048,128]{1,0:T(8,128)(2,1)} %bitcast.11), channel_id=1, source_target_pairs={{0,6},{1,7},{2,0},{3,1},{4,2},{5,3},{6,4},{7,5},{8,14},{9,15},{10,... | collective-permute-start | bytes 1572872 | tf_op jit(solution)/shard_map/ppermute | solution.py:423
  8.1 24.9 %collective-permute-start.3 = (bf16[2048,128]{1,0:T(8,128)(2,1)}, bf16[2048,128]{1,0:T(8,128)(2,1)}, u32[]{:S(2)}, u32[]{:S(2)}) collective-permute-start(bf16[2048,128]{1,0:T(8,128)(2,1)} %bitcast.12), channel_id=1, source_target_pairs={{0,2},{1,3},{2,4},{3,5},{4,6},{5,7},{6,0},{7,1},{8,10},{9,11},{10,... | collective-permute-start | bytes 1572872 | tf_op jit(solution)/shard_map/ppermute | solution.py:423
  11.1 23.6 %all-to-all-start = ((s32[32,8,128]{2,1,0:T(8,128)}), s32[32,8,128]{2,1,0:T(8,128)S(1)}, u32[]{:S(2)}, u32[]{:S(2)}) async-start(s32[32,8,128]{2,1,0:T(8,128)} %get-tuple-element.15), calls=%async_computation | async-start | bytes 262144 | tf_op jit(solution)/shard_map/all_to_all | solution.py:441
  15.3 20.8 %collective-permute-start.2 = (bf16[2048,128]{1,0:T(8,128)(2,1)}, bf16[2048,128]{1,0:T(8,128)(2,1)}, u32[]{:S(2)}, u32[]{:S(2)}) collective-permute-start(bf16[2048,128]{1,0:T(8,128)(2,1)} %bitcast.13), channel_id=1, source_target_pairs={{0,1},{1,0},{2,3},{3,2},{4,5},{5,4},{6,7},{7,6},{8,9},{9,8},{10,11... | collective-permute-start | bytes 1572872 | tf_op jit(solution)/shard_map/ppermute | solution.py:423
  20.8 22.9 %collective-permute-start.8 = (bf16[2048,128]{1,0:T(8,128)(2,1)}, bf16[2048,128]{1,0:T(8,128)(2,1)S(1)}, u32[]{:S(2)}, u32[]{:S(2)}) collective-permute-start(bf16[2048,128]{1,0:T(8,128)(2,1)} %collective-permute-done.5.refs_7_), channel_id=1, source_target_pairs={{0,6},{1,7},{2,0},{3,1},{4,2},{5,3},{6,4},{7,5},{8,14},{9,15},{10,... | collective-permute-start | bytes 1572872 | tf_op jit(solution)/shard_map/ppermute | solution.py:423
  33.0 3.2 %collective-permute-start.6 = (bf16[2048,128]{1,0:T(8,128)(2,1)}, bf16[2048,128]{1,0:T(8,128)(2,1)}, u32[]{:S(2)}, u32[]{:S(2)}) collective-permute-start(bf16[2048,128]{1,0:T(8,128)(2,1)} %collective-permute-done.5.refs_7_), channel_id=1, source_target_pairs={{0,1},{1,0},{2,3},{3,2},{4,5},{5,4},{6,7},{7,6},{8,9},{9,8},{10,11... | collective-permute-start | bytes 1572872 | tf_op jit(solution)/shard_map/ppermute | solution.py:423
  33.0 3.2 %collective-permute-start.4 = (bf16[2048,128]{1,0:T(8,128)(2,1)}, bf16[2048,128]{1,0:T(8,128)(2,1)}, u32[]{:S(2)}, u32[]{:S(2)}) collective-permute-start(bf16[2048,128]{1,0:T(8,128)(2,1)} %collective-permute-done.3.refs_5_), channel_id=1, source_target_pairs={{0,1},{1,0},{2,3},{3,2},{4,5},{5,4},{6,7},{7,6},{8,9},{9,8},{10,11... | collective-permute-start | bytes 1572872 | tf_op jit(solution)/shard_map/ppermute | solution.py:423
  34.8 1.4 %copy-start = (bf16[1,32,128,128]{3,2,1,0:T(8,128)(2,1)S(1)}, bf16[1,32,128,128]{3,2,1,0:T(8,128)(2,1)}, u32[]{:S(2)}) copy-start(bf16[1,32,128,128]{3,2,1,0:T(8,128)(2,1)} %param.7) | copy-start | bytes 3145732
  35.4 14.9 %collective-permute-start.7 = (bf16[4096,128]{1,0:T(8,128)(2,1)S(1)}, bf16[4096,128]{1,0:T(8,128)(2,1)S(1)}, u32[]{:S(2)}, u32[]{:S(2)}) collective-permute-start(bf16[4096,128]{1,0:T(8,128)(2,1)S(1)} %choose.1), channel_id=1, source_target_pairs={{0,8},{1,17},{2,10},{3,19},{4,12},{5,21},{6,14},{7,23},{8,0},{9,25... | collective-permute-start | bytes 3145736 | tf_op jit(solution)/shard_map/ppermute | solution.py:423
  43.7 1.6 %collective-permute-start.9 = (bf16[1024,128]{1,0:T(8,128)(2,1)S(1)}, bf16[1024,128]{1,0:T(8,128)(2,1)S(1)}, u32[]{:S(2)}, u32[]{:S(2)}) collective-permute-start(bf16[1024,128]{1,0:T(8,128)(2,1)S(1)} %get-tuple-element.20.refs_4_), channel_id=1, source_target_pairs={{0,1},{1,0},{2,3},{3,2},{4,5},{5,4},{6,7},{7,6},{8,9},{9,8},{10,11... | collective-permute-start | bytes 786440 | tf_op jit(solution)/shard_map/ppermute | solution.py:423
  45.3 1.5 %collective-permute-start.10 = (bf16[1024,128]{1,0:T(8,128)(2,1)S(1)}, bf16[1024,128]{1,0:T(8,128)(2,1)S(1)}, u32[]{:S(2)}, u32[]{:S(2)}) collective-permute-start(bf16[1024,128]{1,0:T(8,128)(2,1)S(1)} %tied.3.refs_5_), channel_id=1, source_target_pairs={{0,1},{1,0},{2,3},{3,2},{4,5},{5,4},{6,7},{7,6},{8,9},{9,8},{10,11... | collective-permute-start | bytes 786440 | tf_op jit(solution)/shard_map/ppermute | solution.py:423

commit v4 on v3

--- a/solution.py
+++ b/solution.py
@@ -30,7 +30,9 @@
     return device % col_count * row_count + device // col_count
 
 
-def announce_kernel(row_count, col_count, told, ids, out_ref, pos, base, sent):
+def announce_kernel(row_count, col_count, told, ids, piece, out_ref, copy_ref, pos, base, sent, sem):
+    copy = pltpu.make_async_copy(piece, copy_ref, sem)
+    copy.start()
     kept_count = pos.shape[0]
     base[...] = jnp.zeros_like(base)
     base[pl.ds(0, 1), :] = jnp.full((1, LANES), SCAP * out_ref.shape[0], jnp.int32)
@@ -54,21 +56,23 @@
         return carry
 
     lax.fori_loop(0, kept_count, tell, 0)
-
-
-def announce(row_count, col_count, owners, slots, a_ids, b_ids):
+    copy.wait()
+
+
+def announce(row_count, col_count, owners, slots, a_ids, b_ids, piece):
     return pl.pallas_call(
         functools.partial(announce_kernel, row_count, col_count),
         out_shape=[
             pltpu.VMEM((row_count * col_count, EXCHANGE_ROWS, LANES), jnp.int32),
+            pltpu.VMEM(piece.shape, piece.dtype),
             jax.ShapeDtypeStruct(owners.shape, jnp.int32),
         ],
-        in_specs=[SMEM, VMEM],
-        out_specs=[VMEM, SMEM],
-        scratch_shapes=[pltpu.VMEM((EXCHANGE_ROWS, LANES), jnp.int32), pltpu.SMEM((row_count * col_count,), jnp.int32)],
+        in_specs=[SMEM, VMEM, ANY],
+        out_specs=[VMEM, VMEM, SMEM],
+        scratch_shapes=[pltpu.VMEM((EXCHANGE_ROWS, LANES), jnp.int32), pltpu.SMEM((row_count * col_count,), jnp.int32), pltpu.SemaphoreType.DMA],
         compiler_params=limit(2),
         name="announce",
-    )(jnp.concatenate([owners, slots]), jnp.concatenate([a_ids, b_ids], axis=1))
+    )(jnp.concatenate([owners, slots]), jnp.concatenate([a_ids, b_ids], axis=1), piece)
 
 
 def choose_kernel(cuts, where, *refs):
@@ -132,16 +136,16 @@
     pass
 
 
-def tied(array, after):
+def tied(array, *after):
     return pl.pallas_call(
         tie_kernel,
         out_shape=jax.ShapeDtypeStruct(array.shape, array.dtype),
-        in_specs=[ANY] * 2,
+        in_specs=[ANY] * (1 + len(after)),
         out_specs=ANY,
         input_output_aliases={0: 0},
         compiler_params=limit(1),
         name="tied",
-    )(array, after)
+    )(array, *after)
 
 
 class Bringer:
@@ -176,8 +180,10 @@
     bringer.bring("a", refs.pop(0), y * SIDE + SIDE - 1 - x)
     for shift in range(1, y_count):
         bringer.bring("a", refs.pop(0), (y - shift + y_count) % y_count * SIDE + x)
-    for shift in (0, 1, chips - 1):
+    for shift in (0, chips - 1):
         bring_chip(bringer, refs, shift, j, chips)
+    z, core = j // CORES, j % CORES
+    bringer.bring("b", refs.pop(0), (z - 1 + chips) % chips * CORES + core)
 
 
 def bring_rest(bringer, refs, i, j, row_count, col_count):
@@ -189,6 +195,8 @@
     for shift in range(2, chips // 2):
         bring_chip(bringer, refs, shift, j, chips)
         bring_chip(bringer, refs, chips - shift, j, chips)
+    z, core = j // CORES, j % CORES
+    bringer.bring("b", refs.pop(0), (z - 1 + chips) % chips * CORES + CORES - 1 - core)
     bring_chip(bringer, refs, chips // 2, j, chips, PARTS)
 
 
@@ -270,7 +278,8 @@
         source = (half_panel % halves) * row_count + (member + j - i + row_count) % row_count
         a_near = (member % SIDE == i % SIDE) | (member // SIDE == i // SIDE)
         apart = jnp.abs(j // CORES - source // CORES)
-        b_near = (apart <= 1) | (apart == chips - 1)
+        below = (j // CORES - source // CORES + chips) % chips == 1
+        b_near = ((apart <= 1) | (apart == chips - 1)) & ~(below & (j % CORES != source % CORES))
 
         def scan(into, n):
             for slot in range(b_slots):
@@ -415,7 +424,7 @@
     )(plan, recv)
 
 
-def gathered(a_own, b_own, row_count, col_count, where, outgoing, multiply_near):
+def gathered(a_own, b_own, b_copy, row_count, col_count, where, outgoing, multiply_near):
     chips, shifts = col_count // CORES, range(1, row_count // SIDE)
 
     def moved(piece, target):
@@ -434,11 +443,12 @@
     def swapped(piece):
         return moved(piece, lambda d, c: around(d, c, 0, True))
 
-    below = [moved(b_own, lambda d, c: around(d, c, 1))]
+    below = [moved(b_copy, lambda d, c: around(d, c, 1))]
     above = [moved(b_own, lambda d, c: around(d, c, -1))]
     beside = moved(a_own, lambda d, c: (d ^ 1, c))
     ahead = [moved(a_own, lambda d, c, shift=shift: along(d, c, shift)) for shift in shifts]
     exchange = lax.all_to_all(outgoing, ("col", "row"), split_axis=0, concat_axis=0, tiled=True)
+    above[0] = tied(above[0], *ahead)
     for _ in range(2, chips // 2):
         below.append(moved(below[-1], lambda d, c: around(d, c, 1)))
         above.append(moved(above[-1], lambda d, c: around(d, c, -1)))
@@ -450,8 +460,9 @@
     ]
 
     near = [a_own, beside, *ahead]
-    for piece in (b_own, below[0], above[0]):
+    for piece in (b_own, above[0]):
         near += [piece, swapped(piece)]
+    near.append(below[0])
     *buffers, plan = multiply_near(exchange, near)
     opposite = list(cut(tied(opposite, plan)))
     crossed = [swapped(opposite[0])]
@@ -460,7 +471,7 @@
     far = list(diagonal)
     for n in range(1, chips // 2 - 1):
         far += [below[n], swapped(below[n]), above[n], swapped(above[n])]
-    return buffers, plan, far + opposite + crossed
+    return buffers, plan, far + [swapped(below[0])] + opposite + crossed
 
 
 def body(a_blocks, a_rows, b_blocks, b_cols, c_keep, c_owner, c_slot):
@@ -471,11 +482,13 @@
     sizes = (row_count, col_count, b_cols.shape[1])
     where = jnp.stack([lax.axis_index("row"), lax.axis_index("col")]).astype(jnp.int32)
 
-    outgoing, pos = announce(row_count, col_count, owner_ids, slot_ids, a_rows, b_cols)
+    b_own = b_blocks[0].reshape(-1, block)
+    outgoing, b_copy, pos = announce(row_count, col_count, owner_ids, slot_ids, a_rows, b_cols, b_own)
 
     buffers, plan, far = gathered(
         a_blocks[0].reshape(-1, block),
-        b_blocks[0].reshape(-1, block),
+        b_own,
+        b_copy,
         row_count,
         col_count,
         where,

time: 108 us -> 110 us (1.019)
  waiting for transfers between devices: 23.1 us -> 17.8 us
  blocking collectives: 53.7 us -> 56.9 us
  local copies, waits for them, and re-layouts: 0.01 us -> 2.64 us
    ppermute x11, waiting for transfers between devices: 21.9 us -> 17.8 us  [moved(): lax.ppermute(piece, ('row', 'col'), [(d * col_count + c, to[0] * col_coun...]
    all_to_all x1, blocking collectives: 53.7 us -> 56.9 us  [body(): lax.all_to_all(send, ('col', 'row'), split_axis=0, concat_axis=0, tiled=T...]
    unnamed x6 -> x14, local copies, waits for them, and re-layouts: 0.01 us -> 2.64 us
    ppermute x11, starting transfers between devices: 14.1 us -> 16.1 us  [moved(): lax.ppermute(piece, ('row', 'col'), [(d * col_count + c, to[0] * col_coun...]
    all_to_all x1, starting transfers between devices: 4.19 us -> 2.57 us  [gathered(): lax.all_to_all(outgoing, ('col', 'row'), split_axis=0, concat_axis=0, til...]
    all_to_all x1, waiting for transfers between devices: 1.24 us -> 0.01 us  [gathered(): lax.all_to_all(outgoing, ('col', 'row'), split_axis=0, concat_axis=0, til...]
  transfers between devices with their start and end apart: 12 -> 12, of which waited for: 7 -> 6; matrix products, arithmetic and copies ran while one was open for 1% -> 1% of each run, Pallas kernels for 7% -> 7%
where the time goes in v4:
time: 110 us; the launch traced here: 109 us
  blocking collectives  56.9 us (52%)
  starting transfers between devices  18.7 us (17%)
  waiting for transfers between devices  17.8 us (16%)
  Pallas kernels  11.8 us (11%)
  local copies, waits for them, and re-layouts  2.64 us (2%)
  other arithmetic  1.57 us (1%)
    all_to_all x1, blocking collectives, body(): lax.all_to_all(send, ('col', 'row'), split_axis=0, concat_axis=0, tiled=T...  56.9 us
    ppermute x11, waiting for transfers between devices, moved(): lax.ppermute(piece, ('row', 'col'), [(d * col_count + c, to[0] * col_coun...  17.8 us
    ppermute x11, starting transfers between devices, moved(): lax.ppermute(piece, ('row', 'col'), [(d * col_count + c, to[0] * col_coun...  16.1 us
    pallas_call x1, Pallas kernels, first_products(): pl.pallas_call(functools.partial(first_kernel, sizes, len(pieces)), out_s...  4.96 us
    pallas_call x1, Pallas kernels, rest_products(): pl.pallas_call(functools.partial(rest_kernel, sizes, len(pieces)), out_sh...  2.65 us
    unnamed x14, local copies, waits for them, and re-layouts  2.64 us
    all_to_all x1, starting transfers between devices, gathered(): lax.all_to_all(outgoing, ('col', 'row'), split_axis=0, concat_axis=0, til...  2.57 us
  transfers between devices with their start and end apart: 12, of which 6 were waited for; matrix products, arithmetic and copies ran while one was open for 1% of the time, Pallas kernels for 7%

profile of v4, /device:TPU:0, one launch (start us, length us, event | category | flops | bytes accessed | tf_op | source)
XLA Modules:
  0.0 109.5 jit_solution(8321411491290993862)
XLA Ops:
  0.0 3.0 %collective-permute-start.1 = (bf16[4096,128]{1,0:T(8,128)(2,1)}, bf16[4096,128]{1,0:T(8,128)(2,1)S(1)}, u32[]{:S(2)}, u32[]{:S(2)}) collective-permute-start(bf16[4096,128]{1,0:T(8,128)(2,1)} %bitcast.12), channel_id=1, source_target_pairs={{0,16},{1,17},{2,18},{3,19},{4,20},{5,21},{6,22},{7,23},{8,24},{9,... | collective-permute-start | bytes 3145736 | tf_op jit(solution)/shard_map/ppermute | solution.py:432
  3.0 1.5 %collective-permute-start = (bf16[4096,128]{1,0:T(8,128)(2,1)}, bf16[4096,128]{1,0:T(8,128)(2,1)S(1)}, u32[]{:S(2)}, u32[]{:S(2)}) collective-permute-start(bf16[4096,128]{1,0:T(8,128)(2,1)} %bitcast.13), channel_id=1, source_target_pairs={{0,8},{1,9},{2,10},{3,11},{4,12},{5,13},{6,14},{7,15},{8,0},{9,1},... | collective-permute-start | bytes 3145736 | tf_op jit(solution)/shard_map/ppermute | solution.py:432
  4.5 3.6 %collective-permute-start.3 = (bf16[2048,128]{1,0:T(8,128)(2,1)}, bf16[2048,128]{1,0:T(8,128)(2,1)S(1)}, u32[]{:S(2)}, u32[]{:S(2)}) collective-permute-start(bf16[2048,128]{1,0:T(8,128)(2,1)} %bitcast.8), channel_id=1, source_target_pairs={{0,6},{1,7},{2,0},{3,1},{4,2},{5,3},{6,4},{7,5},{8,14},{9,15},{10,... | collective-permute-start | bytes 1572872 | tf_op jit(solution)/shard_map/ppermute | solution.py:432
  8.1 0.7 pad_add_fusion.1.ids
  8.8 0.7 pad_add_fusion.told
  9.6 1.0 copy-done
  10.6 1.6 %announce.1 = (s32[32,8,128]{2,1,0:T(8,128)}, bf16[2048,128]{1,0:T(8,128)(2,1)S(1)}, s32[24]{0:T(128)S(1)}) custom-call(s32[48]{0:T(128)S(1)} %pad_add_fusion.told, s32[1,48]{1,0:T(1,128)S(1)} %pad_add_fusion.1.ids, bf16[2048,128]{1,0:T(8,128)(2,1)S(1)} %bitcast.10), custom_call_target="tpu_custom_call" | custom-call | tf_op jit(solution)/shard_map/announce/pallas_call | solution.py:63
  12.2 0.8 copy-done.6
  13.0 2.6 %all-to-all-start = ((s32[32,8,128]{2,1,0:T(8,128)}), s32[32,8,128]{2,1,0:T(8,128)S(1)}, u32[]{:S(2)}, u32[]{:S(2)}) async-start(s32[32,8,128]{2,1,0:T(8,128)} %get-tuple-element.16), calls=%async_computation | async-start | bytes 262144 | tf_op jit(solution)/shard_map/all_to_all | solution.py:450
  15.8 1.7 %collective-permute-start.5 = (bf16[2048,128]{1,0:T(8,128)(2,1)}, bf16[2048,128]{1,0:T(8,128)(2,1)}, u32[]{:S(2)}, u32[]{:S(2)}) collective-permute-start(bf16[2048,128]{1,0:T(8,128)(2,1)} %copy-done.6), channel_id=1, source_target_pairs={{0,2},{1,3},{2,4},{3,5},{4,6},{5,7},{6,0},{7,1},{8,10},{9,11},{10,... | collective-permute-start | bytes 1572872 | tf_op jit(solution)/shard_map/ppermute | solution.py:432
  17.5 3.3 %collective-permute-done.3.refs_0_ = bf16[2048,128]{1,0:T(8,128)(2,1)S(1)} collective-permute-done((bf16[2048,128]{1,0:T(8,128)(2,1)}, bf16[2048,128]{1,0:T(8,128)(2,1)S(1)}, u32[]{:S(2)}, u32[]{:S(2)}) %collective-permute-start.3) | collective-permute-done | bytes 524320 | tf_op jit(solution)/shard_map/ppermute | solution.py:432
  20.8 6.8 %collective-permute-done.1.refs_1_.refs_2_.refs_0_ = bf16[4096,128]{1,0:T(8,128)(2,1)S(1)} collective-permute-done((bf16[4096,128]{1,0:T(8,128)(2,1)}, bf16[4096,128]{1,0:T(8,128)(2,1)S(1)}, u32[]{:S(2)}, u32[]{:S(2)}) %collective-permute-start.1) | collective-permute-done | bytes 1048608 | tf_op jit(solution)/shard_map/ppermute | solution.py:432
  27.5 0.8 copy-done.2
  28.3 3.9 %collective-permute-start.8 = (bf16[2048,128]{1,0:T(8,128)(2,1)}, bf16[2048,128]{1,0:T(8,128)(2,1)S(1)}, u32[]{:S(2)}, u32[]{:S(2)}) collective-permute-start(bf16[2048,128]{1,0:T(8,128)(2,1)} %copy-done.2), channel_id=1, source_target_pairs={{0,6},{1,7},{2,0},{3,1},{4,2},{5,3},{6,4},{7,5},{8,14},{9,15},{10,... | collective-permute-start | bytes 1572872 | tf_op jit(solution)/shard_map/ppermute | solution.py:432
  32.3 0.6 choose.1
  32.9 1.6 %collective-permute-start.6 = (bf16[4096,128]{1,0:T(8,128)(2,1)S(1)}, bf16[4096,128]{1,0:T(8,128)(2,1)S(1)}, u32[]{:S(2)}, u32[]{:S(2)}) collective-permute-start(bf16[4096,128]{1,0:T(8,128)(2,1)S(1)} %choose.1), channel_id=1, source_target_pairs={{0,8},{1,17},{2,10},{3,19},{4,12},{5,21},{6,14},{7,23},{8,0},{9,25... | collective-permute-start | bytes 3145736 | tf_op jit(solution)/shard_map/ppermute | solution.py:432
  34.5 5.0 %first_products.1 = (bf16[16384,128]{1,0:T(8,128)(2,1)S(1)}, bf16[16384,128]{1,0:T(8,128)(2,1)S(1)}, f32[25,128,128]{2,1,0:T(8,128)S(1)}, s32[356]{0:T(512)S(1)}) custom-call(s32[24]{0:T(128)S(1)} %bitcast.15, s32[24]{0:T(128)S(1)} %get-tuple-element.15.pos, s32[2]{0:T(128)S(1)} %pad_add_fusion.2.where, s32[32,8,128]{2,1,0:T(8,128)S(1)} %all-to-all-done.exchange.refs_2_, ...), custom_call_target="tpu_custom_call" | custom-call | flops 1 | tf_op jit(solution)/shard_map/first_products/pallas_call | solution.py:328
  39.5 5.4 %collective-permute-done.8.refs_0_ = bf16[2048,128]{1,0:T(8,128)(2,1)S(1)} collective-permute-done((bf16[2048,128]{1,0:T(8,128)(2,1)}, bf16[2048,128]{1,0:T(8,128)(2,1)S(1)}, u32[]{:S(2)}, u32[]{:S(2)}) %collective-permute-start.8) | collective-permute-done | bytes 524320 | tf_op jit(solution)/shard_map/ppermute | solution.py:432
  45.5 1.0 collective-permute-done.9.refs_1_.refs_7_
  46.7 0.8 collective-permute-done.7.refs_4_
  47.5 0.6 collective-permute-done.10.refs_8_
  48.1 2.6 %rest_products.1 = (bf16[16384,128]{1,0:T(8,128)(2,1)S(1)}, bf16[16384,128]{1,0:T(8,128)(2,1)S(1)}, f32[25,128,128]{2,1,0:T(8,128)S(1)}, bf16[64,128,128]{2,1,0:T(8,128)(2,1)}) custom-call(s32[356]{0:T(512)S(1)} %get-tuple-element.18.refs_1_.plan, ...), custom_call_target="tpu_custom_call", output_to_operand_aliasing={{0}: (1, {}), {1}: (2, {}), {2}: (3, {})} | custom-call | tf_op jit(solution)/shard_map/rest_products/pallas_call | solution.py:377
  50.7 56.9 %all_to_all.10.recv_ref = bf16[64,128,128]{2,1,0:T(8,128)(2,1)S(1)} all-to-all(bf16[64,128,128]{2,1,0:T(8,128)(2,1)} %get-tuple-element.24), channel_id=1, replica_groups=mesh['row'=4,'col'=8] {'col','row'}, dimensions={0} | all-to-all | bytes 4194304 | tf_op jit(solution)/shard_map/all_to_all | solution.py:499
  107.6 1.9 %place.1 = bf16[64,128,128]{2,1,0:T(8,128)(2,1)} custom-call(s32[356]{0:T(512)S(1)} %get-tuple-element.18.refs_1_.plan, bf16[64,128,128]{2,1,0:T(8,128)(2,1)S(1)} %all_to_all.10.recv_ref), custom_call_target="tpu_custom_call" | custom-call | tf_op jit(solution)/shard_map/place/pallas_call | solution.py:416
  (27 shorter events, 1.1 us)
Async XLA Ops:
  0.0 27.5 %collective-permute-start.1 = (bf16[4096,128]{1,0:T(8,128)(2,1)}, bf16[4096,128]{1,0:T(8,128)(2,1)S(1)}, u32[]{:S(2)}, u32[]{:S(2)}) collective-permute-start(bf16[4096,128]{1,0:T(8,128)(2,1)} %bitcast.12), channel_id=1, source_target_pairs={{0,16},{1,17},{2,18},{3,19},{4,20},{5,21},{6,22},{7,23},{8,24},{9,... | collective-permute-start | bytes 3145736 | tf_op jit(solution)/shard_map/ppermute | solution.py:432
  3.0 29.3 %collective-permute-start = (bf16[4096,128]{1,0:T(8,128)(2,1)}, bf16[4096,128]{1,0:T(8,128)(2,1)S(1)}, u32[]{:S(2)}, u32[]{:S(2)}) collective-permute-start(bf16[4096,128]{1,0:T(8,128)(2,1)} %bitcast.13), channel_id=1, source_target_pairs={{0,8},{1,9},{2,10},{3,11},{4,12},{5,13},{6,14},{7,15},{8,0},{9,1},... | collective-permute-start | bytes 3145736 | tf_op jit(solution)/shard_map/ppermute | solution.py:432
  4.5 16.3 %collective-permute-start.3 = (bf16[2048,128]{1,0:T(8,128)(2,1)}, bf16[2048,128]{1,0:T(8,128)(2,1)S(1)}, u32[]{:S(2)}, u32[]{:S(2)}) collective-permute-start(bf16[2048,128]{1,0:T(8,128)(2,1)} %bitcast.8), channel_id=1, source_target_pairs={{0,6},{1,7},{2,0},{3,1},{4,2},{5,3},{6,4},{7,5},{8,14},{9,15},{10,... | collective-permute-start | bytes 1572872 | tf_op jit(solution)/shard_map/ppermute | solution.py:432
  9.6 1.0 copy-start
  12.2 0.8 copy-start.6
  13.0 19.3 %all-to-all-start = ((s32[32,8,128]{2,1,0:T(8,128)}), s32[32,8,128]{2,1,0:T(8,128)S(1)}, u32[]{:S(2)}, u32[]{:S(2)}) async-start(s32[32,8,128]{2,1,0:T(8,128)} %get-tuple-element.16), calls=%async_computation | async-start | bytes 262144 | tf_op jit(solution)/shard_map/all_to_all | solution.py:450
  15.6 18.9 %collective-permute-start.2 = (bf16[2048,128]{1,0:T(8,128)(2,1)}, bf16[2048,128]{1,0:T(8,128)(2,1)}, u32[]{:S(2)}, u32[]{:S(2)}) collective-permute-start(bf16[2048,128]{1,0:T(8,128)(2,1)} %bitcast.9), channel_id=1, source_target_pairs={{0,1},{1,0},{2,3},{3,2},{4,5},{5,4},{6,7},{7,6},{8,9},{9,8},{10,11... | collective-permute-start | bytes 1572872 | tf_op jit(solution)/shard_map/ppermute | solution.py:432
  15.8 18.7 %collective-permute-start.5 = (bf16[2048,128]{1,0:T(8,128)(2,1)}, bf16[2048,128]{1,0:T(8,128)(2,1)}, u32[]{:S(2)}, u32[]{:S(2)}) collective-permute-start(bf16[2048,128]{1,0:T(8,128)(2,1)} %copy-done.6), channel_id=1, source_target_pairs={{0,2},{1,3},{2,4},{3,5},{4,6},{5,7},{6,0},{7,1},{8,10},{9,11},{10,... | collective-permute-start | bytes 1572872 | tf_op jit(solution)/shard_map/ppermute | solution.py:432
  27.5 0.8 copy-start.2
  28.3 6.2 %copy-start.1 = (bf16[1,16,128,128]{3,2,1,0:T(8,128)(2,1)S(1)}, bf16[1,16,128,128]{3,2,1,0:T(8,128)(2,1)}, u32[]{:S(2)}) copy-start(bf16[1,16,128,128]{3,2,1,0:T(8,128)(2,1)} %param.9) | copy-start | bytes 1572868
  28.3 6.2 %copy-start.5 = (s32[1,1,24]{2,1,0:T(1,128)S(1)}, s32[1,1,24]{2,1,0:T(1,128)}, u32[]{:S(2)}) copy-start(s32[1,1,24]{2,1,0:T(1,128)} %param.11) | copy-start | bytes 292
  28.3 16.6 %collective-permute-start.8 = (bf16[2048,128]{1,0:T(8,128)(2,1)}, bf16[2048,128]{1,0:T(8,128)(2,1)S(1)}, u32[]{:S(2)}, u32[]{:S(2)}) collective-permute-start(bf16[2048,128]{1,0:T(8,128)(2,1)} %copy-done.2), channel_id=1, source_target_pairs={{0,6},{1,7},{2,0},{3,1},{4,2},{5,3},{6,4},{7,5},{8,14},{9,15},{10,... | collective-permute-start | bytes 1572872 | tf_op jit(solution)/shard_map/ppermute | solution.py:432
  32.2 2.3 %collective-permute-start.4 = (bf16[2048,128]{1,0:T(8,128)(2,1)}, bf16[2048,128]{1,0:T(8,128)(2,1)}, u32[]{:S(2)}, u32[]{:S(2)}) collective-permute-start(bf16[2048,128]{1,0:T(8,128)(2,1)} %copy-done.2), channel_id=1, source_target_pairs={{0,1},{1,0},{2,3},{3,2},{4,5},{5,4},{6,7},{7,6},{8,9},{9,8},{10,11... | collective-permute-start | bytes 1572872 | tf_op jit(solution)/shard_map/ppermute | solution.py:432
  32.3 2.2 %copy-start.3 = (bf16[2048,128]{1,0:T(8,128)(2,1)S(1)}, bf16[2048,128]{1,0:T(8,128)(2,1)}, u32[]{:S(2)}) copy-start(bf16[2048,128]{1,0:T(8,128)(2,1)} %copy-done.2) | copy-start | bytes 1572868
  32.3 2.3 %copy-start.4 = (bf16[1,32,128,128]{3,2,1,0:T(8,128)(2,1)S(1)}, bf16[1,32,128,128]{3,2,1,0:T(8,128)(2,1)}, u32[]{:S(2)}) copy-start(bf16[1,32,128,128]{3,2,1,0:T(8,128)(2,1)} %param.7) | copy-start | bytes 3145732
  32.9 15.2 %collective-permute-start.6 = (bf16[4096,128]{1,0:T(8,128)(2,1)S(1)}, bf16[4096,128]{1,0:T(8,128)(2,1)S(1)}, u32[]{:S(2)}, u32[]{:S(2)}) collective-permute-start(bf16[4096,128]{1,0:T(8,128)(2,1)S(1)} %choose.1), channel_id=1, source_target_pairs={{0,8},{1,17},{2,10},{3,19},{4,12},{5,21},{6,14},{7,23},{8,0},{9,25... | collective-permute-start | bytes 3145736 | tf_op jit(solution)/shard_map/ppermute | solution.py:432
  45.0 1.6 %collective-permute-start.9 = (bf16[1024,128]{1,0:T(8,128)(2,1)S(1)}, bf16[1024,128]{1,0:T(8,128)(2,1)S(1)}, u32[]{:S(2)}, u32[]{:S(2)}) collective-permute-start(bf16[1024,128]{1,0:T(8,128)(2,1)S(1)} %get-tuple-element.22.refs_5_), channel_id=1, source_target_pairs={{0,1},{1,0},{2,3},{3,2},{4,5},{5,4},{6,7},{7,6},{8,9},{9,8},{10,11... | collective-permute-start | bytes 786440 | tf_op jit(solution)/shard_map/ppermute | solution.py:432
  45.0 2.5 %collective-permute-start.7 = (bf16[2048,128]{1,0:T(8,128)(2,1)}, bf16[2048,128]{1,0:T(8,128)(2,1)S(1)}, u32[]{:S(2)}, u32[]{:S(2)}) collective-permute-start(bf16[2048,128]{1,0:T(8,128)(2,1)} %collective-permute-done.5.refs_7_), channel_id=1, source_target_pairs={{0,1},{1,0},{2,3},{3,2},{4,5},{5,4},{6,7},{7,6},{8,9},{9,8},{10,11... | collective-permute-start | bytes 1572872 | tf_op jit(solution)/shard_map/ppermute | solution.py:432
  46.6 1.5 %collective-permute-start.10 = (bf16[1024,128]{1,0:T(8,128)(2,1)S(1)}, bf16[1024,128]{1,0:T(8,128)(2,1)S(1)}, u32[]{:S(2)}, u32[]{:S(2)}) collective-permute-start(bf16[1024,128]{1,0:T(8,128)(2,1)S(1)} %tied.5.refs_6_), channel_id=1, source_target_pairs={{0,1},{1,0},{2,3},{3,2},{4,5},{5,4},{6,7},{7,6},{8,9},{9,8},{10,11... | collective-permute-start | bytes 786440 | tf_op jit(solution)/shard_map/ppermute | solution.py:432

commit v5 on v3

--- a/solution.py
+++ b/solution.py
@@ -176,7 +176,7 @@
     bringer.bring("a", refs.pop(0), y * SIDE + SIDE - 1 - x)
     for shift in range(1, y_count):
         bringer.bring("a", refs.pop(0), (y - shift + y_count) % y_count * SIDE + x)
-    for shift in (0, 1, chips - 1):
+    for shift in (0, chips - 1):
         bring_chip(bringer, refs, shift, j, chips)
 
 
@@ -189,6 +189,7 @@
     for shift in range(2, chips // 2):
         bring_chip(bringer, refs, shift, j, chips)
         bring_chip(bringer, refs, chips - shift, j, chips)
+    bring_chip(bringer, refs, 1, j, chips)
     bring_chip(bringer, refs, chips // 2, j, chips, PARTS)
 
 
@@ -269,8 +270,7 @@
         member = half_panel // halves
         source = (half_panel % halves) * row_count + (member + j - i + row_count) % row_count
         a_near = (member % SIDE == i % SIDE) | (member // SIDE == i // SIDE)
-        apart = jnp.abs(j // CORES - source // CORES)
-        b_near = (apart <= 1) | (apart == chips - 1)
+        b_near = (source // CORES - j // CORES + chips) % chips <= 1
 
         def scan(into, n):
             for slot in range(b_slots):
@@ -450,7 +450,7 @@
     ]
 
     near = [a_own, beside, *ahead]
-    for piece in (b_own, below[0], above[0]):
+    for piece in (b_own, above[0]):
         near += [piece, swapped(piece)]
     *buffers, plan = multiply_near(exchange, near)
     opposite = list(cut(tied(opposite, plan)))
@@ -460,7 +460,7 @@
     far = list(diagonal)
     for n in range(1, chips // 2 - 1):
         far += [below[n], swapped(below[n]), above[n], swapped(above[n])]
-    return buffers, plan, far + opposite + crossed
+    return buffers, plan, far + [below[0], swapped(below[0])] + opposite + crossed
 
 
 def body(a_blocks, a_rows, b_blocks, b_cols, c_keep, c_owner, c_slot):
@@ -471,11 +471,12 @@
     sizes = (row_count, col_count, b_cols.shape[1])
     where = jnp.stack([lax.axis_index("row"), lax.axis_index("col")]).astype(jnp.int32)
 
+    b_own = b_blocks[0].reshape(-1, block)
     outgoing, pos = announce(row_count, col_count, owner_ids, slot_ids, a_rows, b_cols)
 
     buffers, plan, far = gathered(
         a_blocks[0].reshape(-1, block),
-        b_blocks[0].reshape(-1, block),
+        b_own,
         row_count,
         col_count,
         where,

time: 108 us -> 106 us (0.981)
  waiting for transfers between devices: 23.1 us -> 20.1 us
    ppermute x11, starting transfers between devices: 14.1 us -> 16.5 us  [moved(): lax.ppermute(piece, ('row', 'col'), [(d * col_count + c, to[0] * col_coun...]
    ppermute x11, waiting for transfers between devices: 21.9 us -> 20.1 us  [moved(): lax.ppermute(piece, ('row', 'col'), [(d * col_count + c, to[0] * col_coun...]
    all_to_all x1, starting transfers between devices: 4.19 us -> 2.59 us  [gathered(): lax.all_to_all(outgoing, ('col', 'row'), split_axis=0, concat_axis=0, til...]
    all_to_all x1, waiting for transfers between devices: 1.24 us -> 0.01 us  [gathered(): lax.all_to_all(outgoing, ('col', 'row'), split_axis=0, concat_axis=0, til...]
    pallas_call x1, Pallas kernels: 2.38 us -> 3.57 us  [rest_products(): pl.pallas_call(functools.partial(rest_kernel, sizes, len(pieces)), out_sh...]
  transfers between devices with their start and end apart: 12 -> 12, of which waited for: 7 -> 6; matrix products, arithmetic and copies ran while one was open for 1% -> 1% of each run, Pallas kernels for 7% -> 6%
where the time goes in v5:
time: 106 us
  blocking collectives  52.9 us (50%)
  waiting for transfers between devices  20.1 us (19%)
  starting transfers between devices  19.1 us (18%)
  Pallas kernels  12.1 us (11%)
  other arithmetic  1.57 us (1%)
    all_to_all x1, blocking collectives, body(): lax.all_to_all(send, ('col', 'row'), split_axis=0, concat_axis=0, tiled=T...  52.9 us
    ppermute x11, waiting for transfers between devices, moved(): lax.ppermute(piece, ('row', 'col'), [(d * col_count + c, to[0] * col_coun...  20.1 us
    ppermute x11, starting transfers between devices, moved(): lax.ppermute(piece, ('row', 'col'), [(d * col_count + c, to[0] * col_coun...  16.5 us
    pallas_call x1, Pallas kernels, first_products(): pl.pallas_call(functools.partial(first_kernel, sizes, len(pieces)), out_s...  4.42 us
    pallas_call x1, Pallas kernels, rest_products(): pl.pallas_call(functools.partial(rest_kernel, sizes, len(pieces)), out_sh...  3.57 us
    all_to_all x1, starting transfers between devices, gathered(): lax.all_to_all(outgoing, ('col', 'row'), split_axis=0, concat_axis=0, til...  2.59 us
  transfers between devices with their start and end apart: 12, of which 6 were waited for; matrix products, arithmetic and copies ran while one was open for 1% of the time, Pallas kernels for 6%

profile of v5, /device:TPU:0, one launch (start us, length us, event | category | flops | bytes accessed | tf_op | source)
XLA Modules:
  0.0 106.0 jit_solution(1423390384011537280)
XLA Ops:
  0.0 3.0 %collective-permute-start.1 = (bf16[4096,128]{1,0:T(8,128)(2,1)}, bf16[4096,128]{1,0:T(8,128)(2,1)S(1)}, u32[]{:S(2)}, u32[]{:S(2)}) collective-permute-start(bf16[4096,128]{1,0:T(8,128)(2,1)} %bitcast.8), channel_id=1, source_target_pairs={{0,16},{1,17},{2,18},{3,19},{4,20},{5,21},{6,22},{7,23},{8,24},{9,... | collective-permute-start | bytes 3145736 | tf_op jit(solution)/shard_map/ppermute | solution.py:423
  3.0 1.5 %collective-permute-start = (bf16[4096,128]{1,0:T(8,128)(2,1)}, bf16[4096,128]{1,0:T(8,128)(2,1)S(1)}, u32[]{:S(2)}, u32[]{:S(2)}) collective-permute-start(bf16[4096,128]{1,0:T(8,128)(2,1)} %bitcast.9), channel_id=1, source_target_pairs={{0,8},{1,9},{2,10},{3,11},{4,12},{5,13},{6,14},{7,15},{8,0},{9,1},... | collective-permute-start | bytes 3145736 | tf_op jit(solution)/shard_map/ppermute | solution.py:423
  4.5 3.6 %collective-permute-start.3 = (bf16[2048,128]{1,0:T(8,128)(2,1)}, bf16[2048,128]{1,0:T(8,128)(2,1)}, u32[]{:S(2)}, u32[]{:S(2)}) collective-permute-start(bf16[2048,128]{1,0:T(8,128)(2,1)} %bitcast.11), channel_id=1, source_target_pairs={{0,6},{1,7},{2,0},{3,1},{4,2},{5,3},{6,4},{7,5},{8,14},{9,15},{10,... | collective-permute-start | bytes 1572872 | tf_op jit(solution)/shard_map/ppermute | solution.py:423
  8.1 0.7 pad_add_fusion.1.ids
  8.8 0.7 pad_add_fusion.told
  9.6 1.6 %announce.1 = (s32[32,8,128]{2,1,0:T(8,128)}, s32[24]{0:T(128)S(1)}) custom-call(s32[48]{0:T(128)S(1)} %pad_add_fusion.told, s32[1,48]{1,0:T(1,128)S(1)} %pad_add_fusion.1.ids), custom_call_target="tpu_custom_call" | custom-call | tf_op jit(solution)/shard_map/announce/pallas_call | solution.py:60
  11.1 2.6 %all-to-all-start = ((s32[32,8,128]{2,1,0:T(8,128)}), s32[32,8,128]{2,1,0:T(8,128)S(1)}, u32[]{:S(2)}, u32[]{:S(2)}) async-start(s32[32,8,128]{2,1,0:T(8,128)} %get-tuple-element.15), calls=%async_computation | async-start | bytes 262144 | tf_op jit(solution)/shard_map/all_to_all | solution.py:441
  13.7 0.2 collective-permute-start.2
  13.9 6.2 %collective-permute-done.3.refs_5_ = bf16[2048,128]{1,0:T(8,128)(2,1)} collective-permute-done((bf16[2048,128]{1,0:T(8,128)(2,1)}, bf16[2048,128]{1,0:T(8,128)(2,1)}, u32[]{:S(2)}, u32[]{:S(2)}) %collective-permute-start.3) | collective-permute-done | bytes 524320 | tf_op jit(solution)/shard_map/ppermute | solution.py:423
  20.1 4.3 %collective-permute-start.8 = (bf16[2048,128]{1,0:T(8,128)(2,1)}, bf16[2048,128]{1,0:T(8,128)(2,1)S(1)}, u32[]{:S(2)}, u32[]{:S(2)}) collective-permute-start(bf16[2048,128]{1,0:T(8,128)(2,1)} %collective-permute-done.3.refs_5_), channel_id=1, source_target_pairs={{0,6},{1,7},{2,0},{3,1},{4,2},{5,3},{6,4},{7,5},{8,14},{9,15},{10,... | collective-permute-start | bytes 1572872 | tf_op jit(solution)/shard_map/ppermute | solution.py:423
  24.4 0.1 pad_add_fusion.2.where
  24.5 3.0 %collective-permute-done.1.refs_2_.refs_0_ = bf16[4096,128]{1,0:T(8,128)(2,1)S(1)} collective-permute-done((bf16[4096,128]{1,0:T(8,128)(2,1)}, bf16[4096,128]{1,0:T(8,128)(2,1)S(1)}, u32[]{:S(2)}, u32[]{:S(2)}) %collective-permute-start.1) | collective-permute-done | bytes 1048608 | tf_op jit(solution)/shard_map/ppermute | solution.py:423
  27.5 1.9 %collective-permute-start.6 = (bf16[2048,128]{1,0:T(8,128)(2,1)}, bf16[2048,128]{1,0:T(8,128)(2,1)}, u32[]{:S(2)}, u32[]{:S(2)}) collective-permute-start(bf16[2048,128]{1,0:T(8,128)(2,1)} %bitcast.13), channel_id=1, source_target_pairs={{0,2},{1,3},{2,4},{3,5},{4,6},{5,7},{6,0},{7,1},{8,10},{9,11},{10,... | collective-permute-start | bytes 1572872 | tf_op jit(solution)/shard_map/ppermute | solution.py:423
  29.4 0.6 choose.1
  30.0 1.6 %collective-permute-start.5 = (bf16[4096,128]{1,0:T(8,128)(2,1)S(1)}, bf16[4096,128]{1,0:T(8,128)(2,1)S(1)}, u32[]{:S(2)}, u32[]{:S(2)}) collective-permute-start(bf16[4096,128]{1,0:T(8,128)(2,1)S(1)} %choose.1), channel_id=1, source_target_pairs={{0,8},{1,17},{2,10},{3,19},{4,12},{5,21},{6,14},{7,23},{8,0},{9,25... | collective-permute-start | bytes 3145736 | tf_op jit(solution)/shard_map/ppermute | solution.py:423
  31.6 4.4 %first_products.1 = (bf16[16384,128]{1,0:T(8,128)(2,1)S(1)}, bf16[16384,128]{1,0:T(8,128)(2,1)S(1)}, f32[25,128,128]{2,1,0:T(8,128)S(1)}, s32[356]{0:T(512)S(1)}) custom-call(s32[24]{0:T(128)S(1)} %bitcast.15, s32[24]{0:T(128)S(1)} %get-tuple-element.14.pos, s32[2]{0:T(128)S(1)} %pad_add_fusion.2.where, s32[32,8,128]{2,1,0:T(8,128)S(1)} %all-to-all-done.exchange.refs_2_, ...), custom_call_target="tpu_custom_call" | custom-call | flops 1 | tf_op jit(solution)/shard_map/first_products/pallas_call | solution.py:319
  36.0 1.0 collective-permute-done.8.refs_0_
  37.2 8.1 %collective-permute-done.6.refs_4_ = bf16[2048,128]{1,0:T(8,128)(2,1)} collective-permute-done((bf16[2048,128]{1,0:T(8,128)(2,1)}, bf16[2048,128]{1,0:T(8,128)(2,1)}, u32[]{:S(2)}, u32[]{:S(2)}) %collective-permute-start.6) | collective-permute-done | bytes 524320 | tf_op jit(solution)/shard_map/ppermute | solution.py:423
  45.3 0.5 collective-permute-start.10
  45.8 1.7 %collective-permute-done.7.refs_5_ = bf16[2048,128]{1,0:T(8,128)(2,1)S(1)} collective-permute-done((bf16[2048,128]{1,0:T(8,128)(2,1)}, bf16[2048,128]{1,0:T(8,128)(2,1)S(1)}, u32[]{:S(2)}, u32[]{:S(2)}) %collective-permute-start.7) | collective-permute-done | bytes 524320 | tf_op jit(solution)/shard_map/ppermute | solution.py:423
  47.5 0.1 collective-permute-done.10.refs_9_
  47.6 3.6 %rest_products.1 = (bf16[16384,128]{1,0:T(8,128)(2,1)S(1)}, bf16[16384,128]{1,0:T(8,128)(2,1)S(1)}, f32[25,128,128]{2,1,0:T(8,128)S(1)}, bf16[64,128,128]{2,1,0:T(8,128)(2,1)}) custom-call(s32[356]{0:T(512)S(1)} %get-tuple-element.16.refs_1_.plan, ...), custom_call_target="tpu_custom_call", output_to_operand_aliasing={{0}: (1, {}), {1}: (2, {}), {2}: (3, {})} | custom-call | tf_op jit(solution)/shard_map/rest_products/pallas_call | solution.py:368
  51.2 52.9 %all_to_all.10.recv_ref = bf16[64,128,128]{2,1,0:T(8,128)(2,1)S(1)} all-to-all(bf16[64,128,128]{2,1,0:T(8,128)(2,1)} %get-tuple-element.22), channel_id=1, replica_groups=mesh['row'=4,'col'=8] {'col','row'}, dimensions={0} | all-to-all | bytes 4194304 | tf_op jit(solution)/shard_map/all_to_all | solution.py:487
  104.1 1.9 %place.1 = bf16[64,128,128]{2,1,0:T(8,128)(2,1)} custom-call(s32[356]{0:T(512)S(1)} %get-tuple-element.16.refs_1_.plan, bf16[64,128,128]{2,1,0:T(8,128)(2,1)S(1)} %all_to_all.10.recv_ref), custom_call_target="tpu_custom_call" | custom-call | tf_op jit(solution)/shard_map/place/pallas_call | solution.py:407
  (18 shorter events, 0.2 us)
Async XLA Ops:
  0.0 31.6 %copy-start.1 = (bf16[1,16,128,128]{3,2,1,0:T(8,128)(2,1)S(1)}, bf16[1,16,128,128]{3,2,1,0:T(8,128)(2,1)}, u32[]{:S(2)}) copy-start(bf16[1,16,128,128]{3,2,1,0:T(8,128)(2,1)} %param.9) | copy-start | bytes 1572868
  0.0 31.6 %copy-start.2 = (s32[1,1,24]{2,1,0:T(1,128)S(1)}, s32[1,1,24]{2,1,0:T(1,128)}, u32[]{:S(2)}) copy-start(s32[1,1,24]{2,1,0:T(1,128)} %param.11) | copy-start | bytes 292
  0.0 27.5 %collective-permute-start.1 = (bf16[4096,128]{1,0:T(8,128)(2,1)}, bf16[4096,128]{1,0:T(8,128)(2,1)S(1)}, u32[]{:S(2)}, u32[]{:S(2)}) collective-permute-start(bf16[4096,128]{1,0:T(8,128)(2,1)} %bitcast.8), channel_id=1, source_target_pairs={{0,16},{1,17},{2,18},{3,19},{4,20},{5,21},{6,22},{7,23},{8,24},{9,... | collective-permute-start | bytes 3145736 | tf_op jit(solution)/shard_map/ppermute | solution.py:423
  3.0 26.4 %collective-permute-start = (bf16[4096,128]{1,0:T(8,128)(2,1)}, bf16[4096,128]{1,0:T(8,128)(2,1)S(1)}, u32[]{:S(2)}, u32[]{:S(2)}) collective-permute-start(bf16[4096,128]{1,0:T(8,128)(2,1)} %bitcast.9), channel_id=1, source_target_pairs={{0,8},{1,9},{2,10},{3,11},{4,12},{5,13},{6,14},{7,15},{8,0},{9,1},... | collective-permute-start | bytes 3145736 | tf_op jit(solution)/shard_map/ppermute | solution.py:423
  4.5 15.6 %collective-permute-start.3 = (bf16[2048,128]{1,0:T(8,128)(2,1)}, bf16[2048,128]{1,0:T(8,128)(2,1)}, u32[]{:S(2)}, u32[]{:S(2)}) collective-permute-start(bf16[2048,128]{1,0:T(8,128)(2,1)} %bitcast.11), channel_id=1, source_target_pairs={{0,6},{1,7},{2,0},{3,1},{4,2},{5,3},{6,4},{7,5},{8,14},{9,15},{10,... | collective-permute-start | bytes 1572872 | tf_op jit(solution)/shard_map/ppermute | solution.py:423
  11.1 18.2 %all-to-all-start = ((s32[32,8,128]{2,1,0:T(8,128)}), s32[32,8,128]{2,1,0:T(8,128)S(1)}, u32[]{:S(2)}, u32[]{:S(2)}) async-start(s32[32,8,128]{2,1,0:T(8,128)} %get-tuple-element.15), calls=%async_computation | async-start | bytes 262144 | tf_op jit(solution)/shard_map/all_to_all | solution.py:441
  13.7 17.8 %collective-permute-start.2 = (bf16[2048,128]{1,0:T(8,128)(2,1)}, bf16[2048,128]{1,0:T(8,128)(2,1)}, u32[]{:S(2)}, u32[]{:S(2)}) collective-permute-start(bf16[2048,128]{1,0:T(8,128)(2,1)} %bitcast.12), channel_id=1, source_target_pairs={{0,1},{1,0},{2,3},{3,2},{4,5},{5,4},{6,7},{7,6},{8,9},{9,8},{10,11... | collective-permute-start | bytes 1572872 | tf_op jit(solution)/shard_map/ppermute | solution.py:423
  20.1 17.0 %collective-permute-start.8 = (bf16[2048,128]{1,0:T(8,128)(2,1)}, bf16[2048,128]{1,0:T(8,128)(2,1)S(1)}, u32[]{:S(2)}, u32[]{:S(2)}) collective-permute-start(bf16[2048,128]{1,0:T(8,128)(2,1)} %collective-permute-done.3.refs_5_), channel_id=1, source_target_pairs={{0,6},{1,7},{2,0},{3,1},{4,2},{5,3},{6,4},{7,5},{8,14},{9,15},{10,... | collective-permute-start | bytes 1572872 | tf_op jit(solution)/shard_map/ppermute | solution.py:423
  24.4 7.2 %collective-permute-start.4 = (bf16[2048,128]{1,0:T(8,128)(2,1)}, bf16[2048,128]{1,0:T(8,128)(2,1)}, u32[]{:S(2)}, u32[]{:S(2)}) collective-permute-start(bf16[2048,128]{1,0:T(8,128)(2,1)} %collective-permute-done.3.refs_5_), channel_id=1, source_target_pairs={{0,1},{1,0},{2,3},{3,2},{4,5},{5,4},{6,7},{7,6},{8,9},{9,8},{10,11... | collective-permute-start | bytes 1572872 | tf_op jit(solution)/shard_map/ppermute | solution.py:423
  27.5 17.8 %collective-permute-start.6 = (bf16[2048,128]{1,0:T(8,128)(2,1)}, bf16[2048,128]{1,0:T(8,128)(2,1)}, u32[]{:S(2)}, u32[]{:S(2)}) collective-permute-start(bf16[2048,128]{1,0:T(8,128)(2,1)} %bitcast.13), channel_id=1, source_target_pairs={{0,2},{1,3},{2,4},{3,5},{4,6},{5,7},{6,0},{7,1},{8,10},{9,11},{10,... | collective-permute-start | bytes 1572872 | tf_op jit(solution)/shard_map/ppermute | solution.py:423
  29.4 2.2 %copy-start = (bf16[1,32,128,128]{3,2,1,0:T(8,128)(2,1)S(1)}, bf16[1,32,128,128]{3,2,1,0:T(8,128)(2,1)}, u32[]{:S(2)}) copy-start(bf16[1,32,128,128]{3,2,1,0:T(8,128)(2,1)} %param.7) | copy-start | bytes 3145732
  30.0 17.6 %collective-permute-start.5 = (bf16[4096,128]{1,0:T(8,128)(2,1)S(1)}, bf16[4096,128]{1,0:T(8,128)(2,1)S(1)}, u32[]{:S(2)}, u32[]{:S(2)}) collective-permute-start(bf16[4096,128]{1,0:T(8,128)(2,1)S(1)} %choose.1), channel_id=1, source_target_pairs={{0,8},{1,17},{2,10},{3,19},{4,12},{5,21},{6,14},{7,23},{8,0},{9,25... | collective-permute-start | bytes 3145736 | tf_op jit(solution)/shard_map/ppermute | solution.py:423
  37.1 8.2 %collective-permute-start.9 = (bf16[1024,128]{1,0:T(8,128)(2,1)S(1)}, bf16[1024,128]{1,0:T(8,128)(2,1)S(1)}, u32[]{:S(2)}, u32[]{:S(2)}) collective-permute-start(bf16[1024,128]{1,0:T(8,128)(2,1)S(1)} %get-tuple-element.20.refs_6_), channel_id=1, source_target_pairs={{0,1},{1,0},{2,3},{3,2},{4,5},{5,4},{6,7},{7,6},{8,9},{9,8},{10,11... | collective-permute-start | bytes 786440 | tf_op jit(solution)/shard_map/ppermute | solution.py:423
  45.3 2.2 %collective-permute-start.7 = (bf16[2048,128]{1,0:T(8,128)(2,1)}, bf16[2048,128]{1,0:T(8,128)(2,1)S(1)}, u32[]{:S(2)}, u32[]{:S(2)}) collective-permute-start(bf16[2048,128]{1,0:T(8,128)(2,1)} %collective-permute-done.6.refs_4_), channel_id=1, source_target_pairs={{0,1},{1,0},{2,3},{3,2},{4,5},{5,4},{6,7},{7,6},{8,9},{9,8},{10,11... | collective-permute-start | bytes 1572872 | tf_op jit(solution)/shard_map/ppermute | solution.py:423
  45.3 2.3 %collective-permute-start.10 = (bf16[1024,128]{1,0:T(8,128)(2,1)S(1)}, bf16[1024,128]{1,0:T(8,128)(2,1)S(1)}, u32[]{:S(2)}, u32[]{:S(2)}) collective-permute-start(bf16[1024,128]{1,0:T(8,128)(2,1)S(1)} %tied.3.refs_7_), channel_id=1, source_target_pairs={{0,1},{1,0},{2,3},{3,2},{4,5},{5,4},{6,7},{7,6},{8,9},{9,8},{10,11... | collective-permute-start | bytes 786440 | tf_op jit(solution)/shard_map/ppermute | solution.py:423
